TPU v7x, 256 devices: a whole 4x4x8 slice. The times are simulated.
256 devices in a mesh: dev: 256 (over y, z, x, core).
Axes of the slice: x: 4, y: 4, z: 8, core: 2. Of those that a mesh axis runs over, the one named last changes fastest.
Arguments:
- states: bfloat16 [1024, 4096], P('dev'), may hold values from -24 to 24
- head_weight: bfloat16 [4096, 1024], replicated, may hold values from -0.25 to 0.25
- bank: bfloat16 [262144, 1024], P('dev'), may hold values from -8 to 8
- positive_index: int32 [1024], P('dev'), may hold values from 0 to 262143
Outputs:
- loss: float32 [], replicated
- top_score: float32 [1024], P('dev')
- grad_states: bfloat16 [1024, 4096], P('dev')
- grad_weight: float32 [4096, 1024], P('dev')
All inputs are finite; a program needn't handle non-finite values.
Results may differ from a plain program's by a relative error of at most 0.012.
The roundings to bfloat16 on the way count: a program that leaves them out, or rounds other values in their place, can miss the bound.
Values may be sent and summed in bfloat16 or wider, within the bound.
A program may use at most 128 MiB of HBM per device.

v0:
```python
import jax
import jax.numpy as jnp
from jax import lax
from jax.sharding import PartitionSpec as P


def local(states, head_weight, bank, positive_index):
    local_queries = states.shape[0]
    bank_rows = bank.shape[0]
    projected = jnp.dot(states, head_weight, preferred_element_type=jnp.float32)
    radius = jnp.sqrt(jnp.sum(projected * projected, axis=1, keepdims=True) + 1e-06)
    unit = projected / radius
    query = unit.astype(jnp.bfloat16)
    all_query, all_positive = (
        lax.all_gather(query, "dev", axis=0, tiled=True),
        lax.all_gather(positive_index, "dev", axis=0, tiled=True),
    )
    query_count = all_query.shape[0]
    offset = lax.axis_index("dev") * bank_rows
    scores = 20.0 * lax.dot_general(
        all_query, bank, (((1,), (1,)), ((), ())), preferred_element_type=jnp.float32
    )
    columns = jnp.arange(bank_rows)
    hits = (all_positive - offset)[:, None] == columns[None, :]
    positive_part = jnp.sum(jnp.where(hits, scores, 0.0), axis=1)
    local_top = jnp.max(scores, axis=1)
    top_score = lax.pmax(local_top, "dev")
    local_total = jnp.sum(jnp.exp(scores - top_score[:, None]), axis=1)
    total, positive = lax.psum((local_total, positive_part), "dev")
    lse = top_score + jnp.log(total)
    loss = jnp.mean(lse - positive)
    block_hits = hits.astype(jnp.float32)
    coef = ((jnp.exp(scores - lse[:, None]) - block_hits) / query_count).astype(jnp.bfloat16)
    grad_query = lax.psum_scatter(
        20.0 * jnp.dot(coef, bank, preferred_element_type=jnp.float32),
        "dev",
        scatter_dimension=0,
        tiled=True,
    )
    inner = jnp.sum(unit * grad_query, axis=1, keepdims=True)
    grad_projected = ((grad_query - unit * inner) / radius).astype(jnp.bfloat16)
    grad_states = lax.dot_general(
        grad_projected, head_weight, (((1,), (1,)), ((), ())), preferred_element_type=jnp.float32
    ).astype(jnp.bfloat16)
    grad_weight = lax.psum_scatter(
        lax.dot_general(
            states, grad_projected, (((0,), (0,)), ((), ())), preferred_element_type=jnp.float32
        ),
        "dev",
        scatter_dimension=0,
        tiled=True,
    )
    own_top = lax.dynamic_slice_in_dim(
        top_score, lax.axis_index("dev") * local_queries, local_queries, 0
    )
    return (loss, own_top, grad_states, grad_weight)


def solution(mesh):
    placed = (P("dev", None), P(), P("dev", None), P("dev"))
    return jax.shard_map(
        local,
        mesh=mesh,
        in_specs=placed,
        out_specs=(P(), P("dev"), P("dev", None), P("dev", None)),
        check_vma=False,
    )
```

profile of v0, /device:TPU:1, one launch (start us, length us, event | category | flops | bytes accessed | tf_op | source)
XLA Modules:
  0.0 1883.6 jit_solution(5921569300236625575)
XLA Ops:
  7.2 0.0 copy-start
  7.2 0.0 copy-start.2
  7.2 0.0 all-gather.3.cloned.1.call-start
  7.2 4.8 multiply_reduce_fusion.2
  12.1 0.7 convert_bitcast_fusion
  12.8 0.0 all-gather.3.cloned.1.call-update
  12.8 0.0 all-reduce.5.cloned.1.call-start
  12.9 0.0 copy-done.2
  12.9 0.2 dynamic-update-slice
  13.1 81.9 %all-reduce = s32[1024]{0:T(1024)S(1)} all-reduce(s32[1024]{0:T(1024)S(1)} %dynamic-update-slice), channel_id=1, replica_groups=mesh['dev'=256] {'dev'}, use_global_device_ids=true, to_apply=%add | all-reduce | flops 1024 | bytes 8192
  95.0 26.2 %all-gather.3.cloned.1.call-done = bf16[256,4,1024]{2,1,0:T(4,128)(2,1)} async-done(((bf16[1,4,1024]{2,1,0:T(4,128)(2,1)}), bf16[256,4,1024]{2,1,0:T(4,128)(2,1)}) %all-gather.3.cloned.1.call-update) | async-done | bytes 2097168 | tf_op jit(solution)/shard_map/all_gather | solution.py:15
  121.2 4.0 reshape.21
  125.1 0.0 copy-done
  125.1 5.9 multiply_reduce_fusion
  131.0 76.7 %pmax.7 = f32[1024]{0:T(1024)S(1)} all-reduce(f32[1024]{0:T(1024)S(1)} %get-tuple-element.20), channel_id=1, replica_groups=mesh['dev'=256] {'dev'}, use_global_device_ids=true, to_apply=%region_2.3 | all-reduce | flops 1024 | bytes 8192 | tf_op jit(solution)/shard_map/pmax | solution.py:27
  207.8 3.4 select_reduce_fusion
  211.2 72.7 %all-reduce.2 = (f32[1024]{0:T(1024)S(1)}, f32[1024]{0:T(1024)S(1)}) all-reduce(f32[1024]{0:T(1024)S(1)} %get-tuple-element.13, f32[1024]{0:T(1024)S(1)} %get-tuple-element.12), channel_id=1, replica_groups=mesh['dev'=256] {'dev'}, use_global_device_ids=true, to_apply=%region_4.5 | all-reduce | flops 2048 | bytes 16384 | tf_op jit(solution)/shard_map/psum | solution.py:29
  283.9 0.6 subtract_reduce_fusion
  284.5 6.7 convolution_multiply_fusion
  291.2 5.3 copy.11
  296.5 0.0 copy-start.1
  296.5 0.0 all-reduce.5.cloned.1.call-update
  296.6 0.2 reduce-scatter.4.cloned.1.call-start
  296.8 262.5 %all-reduce.5.cloned.1.call-done = f32[1024,1024]{1,0:T(8,128)} async-done(((f32[1024,1024]{1,0:T(8,128)}), f32[1024,1024]{1,0:T(8,128)}) %all-reduce.5.cloned.1.call-update) | async-done | bytes 4194320
  559.3 0.9 multiply_reduce_fusion.1
  560.3 0.0 copy-done.1
  560.3 8.9 convolution_bitcast_fusion
  569.2 17.5 copy.14
  586.7 0.0 reduce-scatter.4.cloned.1.call-update
  586.7 0.6 dynamic_slice.3
  587.9 6.3 convolution_convert_fusion
  594.2 1281.7 %reduce-scatter.4.cloned.1.call-done = f32[16,1024]{1,0:T(8,128)} async-done(((f32[4096,1024]{1,0:T(8,128)}), f32[16,1024]{1,0:T(8,128)}) %reduce-scatter.4.cloned.1.call-update) | async-done | bytes 65552
  (3 shorter events, 0.0 us)
Async XLA Ops:
  7.2 118.0 %copy-start = (bf16[1024,1024]{1,0:T(8,128)(2,1)S(1)}, bf16[1024,1024]{1,0:T(8,128)(2,1)}, u32[]{:S(2)}) copy-start(bf16[1024,1024]{1,0:T(8,128)(2,1)} %param.6) | copy-start | bytes 6291460
  7.2 5.7 copy-start.2
  7.2 114.0 %all-gather.3.cloned.1.call-start = ((), (), s32[]{:S(2)}) async-start(), calls=%async_computation.1 | async-start | bytes 2105344 | tf_op jit(solution)/shard_map/all_gather | solution.py:15
  12.8 546.5 %all-reduce.5.cloned.1.call-start = ((), (), s32[]{:S(2)}) async-start(), calls=%async_computation.3 | async-start | bytes 8388608
  296.5 263.7 %copy-start.1 = (bf16[4,4096]{1,0:T(4,128)(2,1)S(1)}, bf16[4,4096]{1,0:T(4,128)(2,1)}, u32[]{:S(2)}) copy-start(bf16[4,4096]{1,0:T(4,128)(2,1)} %param.4) | copy-start | bytes 98308
  296.6 1579.4 %reduce-scatter.4.cloned.1.call-start = ((), (), s32[]{:S(2)}) async-start(), calls=%async_computation.2 | async-start | bytes 16842752
Sparse Core Ops, SparseCore 0:
  12.9 108.2 all-gather.2
  296.7 262.5 all-reduce.4
  586.8 1289.1 reduce-scatter.3
where the time goes:
time: 1890 us; the launch traced here: 1880 us
  waiting for transfers between devices  1570 us (83%)
  blocking collectives  231 us (12%)
  matrix products  32.7 us (2%)
  local copies, waits for them, and re-layouts  27.6 us (1%)
    unnamed x5, waiting for transfers between devices  1540 us
    unnamed x1, blocking collectives  81.9 us
    pmax x1, blocking collectives, local(): top_score = lax.pmax(local_top, 'dev')  76.7 us
    psum x1, blocking collectives, local(): total, positive = lax.psum((local_total, positive_part), 'dev')  72.7 us
  transfers between devices with their start and end apart: 3, of which 3 were waited for; matrix products, arithmetic and copies ran while one was open for 0% of the time, Pallas kernels for 0%

commit v1 on v0

v1 whole, which is shorter than its diff:
```python
import functools

import jax
import jax.numpy as jnp
from jax import lax
from jax.experimental import pallas as pl
from jax.experimental.pallas import tpu as pltpu
from jax.sharding import PartitionSpec as P

NY, NZ, NX = 4, 8, 4
PLANE = NY * NX
OWN = 4
H, E = 4096, 1024
BANK = 1024
BLOCK = NZ * OWN
CHUNK = NX * BLOCK
ROWS = NY * CHUNK
LANES = 128
SPLIT = E // LANES
W_PARTS = 8
QUERIES = 1024
MESH = pl.DeviceIdType.MESH
NT = (((1,), (1,)), ((), ()))
POS, STATES, QUERY, STATS, GRAD, PROJ = range(6)
F32, BF16 = jnp.float32, jnp.bfloat16


def kernel(
    states_ref, w_hbm, bank_hbm, pos_ref,
    loss_ref, top_ref, gs_ref, gw_ref,
    w, bank, posz, posp, stz_out, stz_in, stp_out, slab, slab_t, turn,
    zq, unit_s, radius_s, qall, expo, coef, sp, sz, final, gout, gin,
    gz_out, gz_in, zg, own_gp, gpall, gw_acc, gw_in, lossbuf,
    w_sem, bank_sem, cs, cr, zs, zr, ps, pr,
):
    me = lax.axis_index("dev")
    c = lax.rem(me, 2)
    x = lax.rem(me // 2, NX)
    z = lax.rem(me // (2 * NX), NZ)
    y = me // (2 * NX * NZ)
    p = y * NX + x
    chip = me // 2
    partner = chip * 2 + (1 - c)

    def dev(yy, zz, xx):
        return ((yy * NZ + zz) * NX + xx) * 2 + c

    def rows(i, n):
        return pl.ds(pl.multiple_of(i * n, n), n)

    def z_copy(stage, t, src, dst, slot):
        return pltpu.make_async_remote_copy(
            src_ref=src, dst_ref=dst, send_sem=zs.at[stage, t], recv_sem=zr.at[stage, slot],
            device_id=(dev(y, t, x),), device_id_type=MESH,
        )

    def p_copy(stage, t, src, dst, slot):
        return pltpu.make_async_remote_copy(
            src_ref=src, dst_ref=dst, send_sem=ps.at[stage, t], recv_sem=pr.at[stage, slot],
            device_id=(dev(t // NX, z, lax.rem(t, NX)),), device_id_type=MESH,
        )

    def z_each(body):
        def step(k, carry):
            body(lax.rem(z + k, NZ))
            return carry
        lax.fori_loop(1, NZ, step, 0)

    def p_peer(k):
        return lax.rem(y + k // NX, NY) * NX + lax.rem(x + lax.rem(k, NX), NX)

    def p_each(body, first=1, last=PLANE):
        def step(k, carry):
            body(p_peer(k))
            return carry
        lax.fori_loop(first, last, step, 0)

    def z_send(stage, src, dst):
        z_each(lambda t: z_copy(stage, t, src(t), dst(z), z).start())

    def z_recv(stage, dst):
        z_each(lambda t: z_copy(stage, t, dst(t), dst(t), t).wait_recv())

    def z_drain(stage, src):
        z_each(lambda t: z_copy(stage, t, src(t), src(t), t).wait_send())

    def p_send(stage, src, dst):
        p_each(lambda t: p_copy(stage, t, src(t), dst(p), p).start())

    def p_recv(stage, dst, first=1, last=PLANE):
        p_each(lambda t: p_copy(stage, t, dst(t), dst(t), t).wait_recv(), first, last)

    def p_drain(stage, src):
        p_each(lambda t: p_copy(stage, t, src(t), src(t), t).wait_send())

    def w_copy(i):
        part = pl.ds(i * (H // W_PARTS), H // W_PARTS)
        return pltpu.make_async_copy(w_hbm.at[part, :], w.at[part, :], w_sem.at[i])

    for i in range(W_PARTS):
        w_copy(i).start()
    mine = rows(c, BANK)
    other = rows(1 - c, BANK)
    own_bank = pltpu.make_async_copy(bank_hbm, bank.at[mine, :], bank_sem)
    own_bank.start()

    barrier = pltpu.get_barrier_semaphore()

    def greet(target):
        pl.semaphore_signal(barrier, inc=1, device_id=(target,), device_id_type=MESH)

    greet(partner)
    z_each(lambda t: greet(dev(y, t, x)))
    p_each(lambda t: greet(dev(t // NX, z, lax.rem(t, NX))))
    lane = lax.broadcasted_iota(jnp.int32, (8, LANES), 1)
    sub = lax.broadcasted_iota(jnp.int32, (8, LANES), 0)
    first_lane = x * BLOCK + z * OWN
    tile = jnp.zeros((8, LANES), jnp.int32)
    for r in range(OWN):
        tile = jnp.where((lane == first_lane + r) & (sub == y), pos_ref[r], tile)
    posz[rows(z, 8), :] = tile
    states_f = states_ref[...].astype(F32)
    for zz in range(NZ):
        for yy in range(NY):
            at = (yy * NZ + zz) * LANES
            stz_out[pl.ds(zz * 16 + yy, OWN, stride=NY), :] = states_f[:, at:at + LANES]
    pl.semaphore_wait(barrier, 1 + (NZ - 1) + (PLANE - 1))

    def core_copy(i, src, dst):
        return pltpu.make_async_remote_copy(
            src_ref=src, dst_ref=dst, send_sem=cs.at[i], recv_sem=cr.at[i],
            device_id=(partner,), device_id_type=MESH,
        )

    bank_out = core_copy(0, bank_hbm, bank.at[mine, :])
    bank_out.start()

    z_send(POS, lambda t: posz.at[rows(z, 8), :], lambda s: posz.at[rows(s, 8), :])
    stz_in[rows(z, 16), :] = stz_out[rows(z, 16), :]
    z_send(STATES, lambda t: stz_out.at[rows(t, 16), :], lambda s: stz_in.at[rows(s, 16), :])

    proj = jnp.zeros((OWN, E), F32)
    for i in range(W_PARTS):
        w_copy(i).wait()
        part = slice(i * (H // W_PARTS), (i + 1) * (H // W_PARTS))
        proj = proj + jnp.dot(states_ref[:, part], w[part, :], preferred_element_type=F32)
    radius = jnp.sqrt(jnp.sum(proj * proj, axis=1, keepdims=True) + 1e-06)
    unit = proj / radius
    for e in range(SPLIT):
        unit_s[pl.ds(e, OWN, stride=SPLIT), :] = unit[:, e * LANES:(e + 1) * LANES]
    radius_b = jnp.broadcast_to(radius, (OWN, LANES))
    for e in range(SPLIT):
        radius_s[pl.ds(e, OWN, stride=SPLIT), :] = radius_b
    zq[rows(z, BLOCK), :] = unit_s[...]
    zq_at = lambda s: zq.at[rows(s, BLOCK), :]
    z_send(QUERY, lambda t: zq_at(z), zq_at)

    z_recv(POS, lambda s: posz.at[rows(s, 8), :])
    tile = jnp.zeros((8, LANES), jnp.int32)
    for s in range(NZ):
        tile = tile + posz[s * 8:(s + 1) * 8, :]
    posp[rows(p, 8), :] = tile
    posp_at = lambda s: posp.at[rows(s, 8), :]
    p_send(POS, lambda t: posp_at(p), posp_at)
    z_recv(STATES, lambda s: stz_in.at[rows(s, 16), :])
    for yy in range(NY):
        stp_out[yy * BLOCK:(yy + 1) * BLOCK, :] = stz_in[pl.ds(yy, BLOCK, stride=NY), :].astype(BF16)
    block_at = lambda ref: (lambda s: ref.at[rows(s, BLOCK), :])
    st_src = lambda t: stp_out.at[rows(t // NX, BLOCK), :]

    z_recv(QUERY, zq_at)

    def assemble(zbuf, target):
        for e in range(SPLIT):
            target[rows(p, BLOCK), e * LANES:(e + 1) * LANES] = zbuf[pl.ds(e, BLOCK, stride=SPLIT), :].astype(BF16)

    assemble(zq, qall)
    p_send(QUERY, lambda t: block_at(qall)(p), block_at(qall))
    p_send(STATES, st_src, block_at(slab))
    slab[rows(p, BLOCK), :] = stp_out[rows(y, BLOCK), :]
    own_bank.wait()
    core_copy(0, bank.at[other, :], bank.at[other, :]).wait_recv()
    p_recv(POS, posp_at)
    tile = jnp.zeros((8, LANES), jnp.int32)
    for s in range(PLANE):
        tile = tile + posp[s * 8:(s + 1) * 8, :]
    final[16:24, :] = (tile - chip * (2 * BANK)).astype(F32)

    eye = lax.broadcasted_iota(jnp.int32, (LANES, LANES), 0) == lax.broadcasted_iota(jnp.int32, (LANES, LANES), 1)
    to_row = lambda col: jnp.sum(jnp.where(eye, jnp.broadcast_to(col, (LANES, LANES)), 0.0), axis=0, keepdims=True)
    to_col = lambda row: jnp.sum(jnp.where(eye, jnp.broadcast_to(row, (LANES, LANES)), 0.0), axis=1, keepdims=True)
    TILE = 512
    tiles = 2 * BANK // TILE
    column = lax.broadcasted_iota(jnp.int32, (CHUNK, TILE), 1)

    sp[rows(p, 16), :] = jnp.zeros((16, LANES), F32)

    def score_chunk(k, carry):
        yy = lax.rem(y + k, NY)
        p_recv(QUERY, block_at(qall), jnp.maximum(k * NX, 1), (k + 1) * NX)
        at = rows(yy, CHUNK)
        hit_col = to_col(final[pl.ds(16 + yy, 1), :]).astype(jnp.int32)
        top = jnp.full((CHUNK, 1), -jnp.inf, F32)
        positive = jnp.zeros((1, LANES), F32)
        for j in range(tiles):
            here = slice(j * TILE, (j + 1) * TILE)
            scores = 20.0 * lax.dot_general(qall[at, :], bank[here, :], NT, preferred_element_type=F32)
            expo[at, here] = scores
            top = jnp.maximum(top, jnp.max(scores, axis=1, keepdims=True))
            found = jnp.sum(jnp.where(column == hit_col - j * TILE, scores, 0.0), axis=0, keepdims=True)
            for g in range(TILE // LANES):
                positive = positive + found[:, g * LANES:(g + 1) * LANES]
        total = jnp.zeros((CHUNK, 1), F32)
        for j in range(tiles):
            here = slice(j * TILE, (j + 1) * TILE)
            value = jnp.exp(expo[at, here] - top)
            expo[at, here] = value
            total = total + jnp.sum(value, axis=1, keepdims=True)
        base = p * 16
        sp[pl.ds(base + yy, 1), :] = to_row(top)
        sp[pl.ds(base + 8 + yy, 1), :] = to_row(total)
        sp[pl.ds(base + 4, 1), :] += positive
        return carry

    lax.fori_loop(0, NY, score_chunk, 0)

    sp_at = lambda s: sp.at[rows(s, 16), :]
    sz_at = lambda s: sz.at[rows(s, 16), :]
    final[0:8, :] = sp[pl.ds(pl.multiple_of(p * 16, 16), 8), :]

    def combine(ref, n):
        high = ref[0:8, :]
        found = high
        for s in range(1, n):
            part = ref[s * 16:s * 16 + 8, :]
            high = jnp.maximum(high, part)
            found = found + part
        total = jnp.zeros((8, LANES), F32)
        for s in range(n):
            total = total + ref[s * 16 + 8:s * 16 + 16, :] * jnp.exp(ref[s * 16:s * 16 + 8, :] - high)
        return high, found, total

    p_send(STATS, lambda t: sp_at(p), sp_at)
    p_recv(STATS, sp_at)
    high, found, total = combine(sp, PLANE)
    mid = pl.multiple_of(z * 16, 16)
    sz[pl.ds(mid, 8), :] = jnp.where(sub < 4, high, found)
    sz[pl.ds(mid + 8, 8), :] = total
    z_send(STATS, lambda t: sz_at(z), sz_at)
    z_recv(STATS, sz_at)
    high, found, total = combine(sz, NZ)
    lse = high + jnp.log(jnp.where(sub < 4, total, 1.0))
    per_lane = jnp.where(sub < 4, lse, jnp.where(sub == 4, -found, 0.0))
    lossbuf[0:8, :] = jnp.broadcast_to(jnp.sum(per_lane), (8, LANES))
    loss_out = core_copy(1, lossbuf.at[0:8, :], lossbuf.at[8:16, :])
    loss_out.start()
    scale = jnp.exp(final[0:8, :] - lse)
    final[8:16, :] = scale
    final[24:32, :] = high
    top_row = pltpu.roll(final[pl.ds(24 + y, 1), :], lax.rem(LANES - first_lane, LANES), 1)
    top_ref[...] = top_row[:, :OWN]

    def grad_chunk(i, carry):
        k = lax.rem(i + 1, NY)
        yy = lax.rem(y + k, NY)
        at = rows(yy, CHUNK)
        hit_col = to_col(final[pl.ds(16 + yy, 1), :]).astype(jnp.int32)
        scale_col = to_col(final[pl.ds(8 + yy, 1), :])
        for j in range(tiles):
            here = slice(j * TILE, (j + 1) * TILE)
            hits = (column == hit_col - j * TILE).astype(F32)
            coef[:, here] = ((expo[at, here] * scale_col - hits) * (1.0 / QUERIES)).astype(BF16)
        for j in range(E // TILE):
            here = slice(j * TILE, (j + 1) * TILE)
            value = 20.0 * jnp.dot(coef[...], bank[:, here], preferred_element_type=F32)
            gout[at, here] = value.astype(BF16)
        p_each(
            lambda t: p_copy(GRAD, t, block_at(gout)(t), block_at(gin)(p), p).start(),
            jnp.maximum(k * NX, 1), (k + 1) * NX,
        )
        return carry

    lax.fori_loop(0, NY, grad_chunk, 0)
    gin[rows(p, BLOCK), :] = gout[rows(p, BLOCK), :]

    p_recv(STATES, block_at(slab))
    for yy in range(NY):
        turn[...] = jnp.transpose(slab[yy * CHUNK:(yy + 1) * CHUNK, :].astype(F32))
        slab_t[yy] = turn[rows(x, 32), :].astype(BF16)

    acc = gin[rows(p, BLOCK), :].astype(F32)

    def gather(k, acc):
        t = p_peer(k)
        there = block_at(gin)(t)
        p_copy(GRAD, t, there, there, t).wait_recv()
        return acc + gin[rows(t, BLOCK), :].astype(F32)

    acc = lax.fori_loop(1, PLANE, lambda i, a: gather(lax.rem(i + 3, 15) + 1, a), acc)
    for e in range(SPLIT):
        gz_out[pl.ds(e, BLOCK, stride=SPLIT), :] = acc[:, e * LANES:(e + 1) * LANES]
    gz_in[rows(z, BLOCK), :] = gz_out[rows(z, BLOCK), :]
    z_send(GRAD, lambda t: gz_out.at[rows(t, BLOCK), :], lambda s: gz_in.at[rows(s, BLOCK), :])
    z_recv(GRAD, lambda s: gz_in.at[rows(s, BLOCK), :])
    grad = gz_in[0:BLOCK, :]
    for s in range(1, NZ):
        grad = grad + gz_in[s * BLOCK:(s + 1) * BLOCK, :]
    for r in range(OWN):
        one = slice(r * SPLIT, (r + 1) * SPLIT)
        g, u = grad[one, :], unit_s[one, :]
        inner = jnp.sum(jnp.sum(u * g, axis=1, keepdims=True), axis=0, keepdims=True)
        own_gp[one, :] = ((g - u * inner) / radius_s[one, :]).astype(BF16).astype(F32)
    zg[rows(z, BLOCK), :] = own_gp[...]
    zg_at = lambda s: zg.at[rows(s, BLOCK), :]
    z_send(PROJ, lambda t: zg_at(z), zg_at)

    gp = jnp.concatenate(
        [own_gp[pl.ds(e, OWN, stride=SPLIT), :] for e in range(SPLIT)], axis=1
    ).astype(BF16)
    for j in range(H // TILE):
        here = slice(j * TILE, (j + 1) * TILE)
        gs_ref[:, here] = lax.dot_general(gp, w[here, :], NT, preferred_element_type=F32).astype(BF16)

    z_recv(PROJ, zg_at)
    assemble(zg, gpall)
    p_send(PROJ, lambda t: block_at(gpall)(p), block_at(gpall))
    gw_acc[...] = jnp.zeros_like(gw_acc)

    def weight_chunk(k, carry):
        yy = lax.rem(y + k, NY)
        p_recv(PROJ, block_at(gpall), jnp.maximum(k * NX, 1), (k + 1) * NX)
        gw_acc[...] += jnp.dot(slab_t[yy], gpall[rows(yy, CHUNK), :], preferred_element_type=F32)
        return carry

    lax.fori_loop(0, NY, weight_chunk, 0)
    gw_out = core_copy(2, gw_acc.at[rows(1 - c, 16), :], gw_in)
    gw_out.start()
    core_copy(1, lossbuf.at[0:8, :], lossbuf.at[8:16, :]).wait_recv()
    loss_ref[...] = ((lossbuf[0:1, 0:1] + lossbuf[8:9, 0:1]) * (1.0 / QUERIES))
    z_drain(POS, lambda t: posz.at[rows(z, 8), :])
    z_drain(STATES, lambda t: stz_out.at[rows(t, 16), :])
    z_drain(QUERY, lambda t: zq_at(z))
    z_drain(STATS, lambda t: sz_at(z))
    z_drain(GRAD, lambda t: gz_out.at[rows(t, BLOCK), :])
    z_drain(PROJ, lambda t: zg_at(z))
    p_drain(POS, lambda t: posp_at(p))
    p_drain(STATES, st_src)
    p_drain(QUERY, lambda t: block_at(qall)(p))
    p_drain(STATS, lambda t: sp_at(p))
    p_drain(GRAD, lambda t: block_at(gout)(t))
    p_drain(PROJ, lambda t: block_at(gpall)(p))
    bank_out.wait_send()
    loss_out.wait_send()
    gw_out.wait_send()
    gw_out.wait_recv()
    gw_ref[...] = gw_acc[rows(c, 16), :] + gw_in[...]


def local(states, head_weight, bank, positive_index):
    vmem = pltpu.VMEM
    dma = pltpu.SemaphoreType.DMA
    in_vmem = pl.BlockSpec(memory_space=pltpu.VMEM)
    loss, top, grad_states, grad_weight = pl.pallas_call(
        kernel,
        out_shape=(
            jax.ShapeDtypeStruct((1, 1), F32),
            jax.ShapeDtypeStruct((1, OWN), F32),
            jax.ShapeDtypeStruct((OWN, H), BF16),
            jax.ShapeDtypeStruct((16, E), F32),
        ),
        in_specs=[
            in_vmem,
            pl.BlockSpec(memory_space=pl.ANY),
            pl.BlockSpec(memory_space=pl.ANY),
            pl.BlockSpec(memory_space=pltpu.SMEM),
        ],
        out_specs=(in_vmem,) * 4,
        scratch_shapes=[
            vmem((H, E), BF16),
            vmem((2 * BANK, E), BF16),
            vmem((NZ * 8, LANES), jnp.int32),
            vmem((PLANE * 8, LANES), jnp.int32),
            vmem((NZ * 16, LANES), F32),
            vmem((NZ * 16, LANES), F32),
            vmem((NY * BLOCK, LANES), BF16),
            vmem((ROWS, LANES), BF16),
            vmem((NY, 32, CHUNK), BF16),
            vmem((LANES, CHUNK), F32),
            vmem((NZ * BLOCK, LANES), F32),
            vmem((BLOCK, LANES), F32),
            vmem((BLOCK, LANES), F32),
            vmem((ROWS, E), BF16),
            vmem((ROWS, 2 * BANK), F32),
            vmem((CHUNK, 2 * BANK), BF16),
            vmem((PLANE * 16, LANES), F32),
            vmem((NZ * 16, LANES), F32),
            vmem((32, LANES), F32),
            vmem((ROWS, E), BF16),
            vmem((ROWS, E), BF16),
            vmem((NZ * BLOCK, LANES), F32),
            vmem((NZ * BLOCK, LANES), F32),
            vmem((NZ * BLOCK, LANES), F32),
            vmem((BLOCK, LANES), F32),
            vmem((ROWS, E), BF16),
            vmem((32, E), F32),
            vmem((16, E), F32),
            vmem((16, LANES), F32),
            dma((W_PARTS,)), dma,
            dma((3,)), dma((3,)),
            dma((6, NZ)), dma((6, NZ)),
            dma((6, PLANE)), dma((6, PLANE)),
        ],
        compiler_params=pltpu.CompilerParams(
            collective_id=0, has_side_effects=True, vmem_limit_bytes=56 * 2**20
        ),
        name="info_nce",
    )(states, head_weight, bank, positive_index)
    return (loss.reshape(()), top.reshape((OWN,)), grad_states, grad_weight)


def solution(mesh):
    placed = (P("dev", None), P(), P("dev", None), P("dev"))
    return jax.shard_map(
        local,
        mesh=mesh,
        in_specs=placed,
        out_specs=(P(), P("dev"), P("dev", None), P("dev", None)),
        check_vma=False,
    )
```

time: 1890 us -> 99.2 us (0.05)
  waiting for transfers between devices: 1570 us -> 0 us
  blocking collectives: 231 us -> 0 us
  Pallas kernels: 0 us -> 92.3 us
  matrix products: 32.7 us -> 0 us
  local copies, waits for them, and re-layouts: 27.6 us -> 3.96 us
    unnamed x5 -> x0, waiting for transfers between devices: 1540 us -> none
    pallas_call x0 -> x1, Pallas kernels: none -> 92.3 us  [local(): pl.pallas_call(kernel, out_shape=(jax.ShapeDtypeStruct((1, 1), F32), jax....]
    unnamed x1 -> x0, blocking collectives: 81.9 us -> none
    pmax x1 -> x0, blocking collectives: 76.7 us -> none  [local(): top_score = lax.pmax(local_top, 'dev')]
    psum x1 -> x0, blocking collectives: 72.7 us -> none  [local(): total, positive = lax.psum((local_total, positive_part), 'dev')]
    dot_general x5 -> x0, matrix products: 32.7 us -> none  [the longest x1 8.93 us: local(): lax.dot_general(states, grad_projected, (((0,), (0,)), ((), ())), preferr...]
    all_gather x1 -> x0, waiting for transfers between devices: 26.2 us -> none  [local(): lax.all_gather(query, 'dev', axis=0, tiled=True)]
  transfers between devices with their start and end apart: 3 -> 0, of which waited for: 3 -> 0; matrix products, arithmetic and copies ran while one was open for 0% -> 0% of each run, Pallas kernels for 0% -> 0%
where the time goes in v1:
time: 99.2 us; the launch traced here: 98.8 us
  Pallas kernels  92.3 us (93%)
  local copies, waits for them, and re-layouts  3.96 us (4%)
  between operations  2.46 us (2%)
    pallas_call x1, Pallas kernels, local(): pl.pallas_call(kernel, out_shape=(jax.ShapeDtypeStruct((1, 1), F32), jax....  92.3 us
    unnamed x3, local copies, waits for them, and re-layouts  3.96 us

profile of v1, /device:TPU:1, one launch (start us, length us, event | category | flops | bytes accessed | tf_op | source)
XLA Modules:
  0.0 98.8 jit_solution(6172917448712121427)
XLA Ops:
  0.6 92.3 %info_nce.1 = (f32[1,1]{1,0:T(1,128)}, f32[1,4]{1,0:T(1,128)}, bf16[4,4096]{1,0:T(4,128)(2,1)}, f32[16,1024]{1,0:T(8,128)}) custom-call(bf16[4,4096]{1,0:T(4,128)(2,1)} %states_ref.1, bf16[4096,1024]{1,0:T(8,128)(2,1)} %w_hbm.1, bf16[1024,1024]{1,0:T(8,128)(2,1)} %bank_hbm.1, s32[4]{0:T(128)} %pos_ref.1), custom_call_target="tpu_custom_call" | custom-call | tf_op jit(solution)/shard_map/info_nce/pallas_call | solution.py:363
  93.7 1.1 %copy.13 = f32[4]{0:T(128)} copy(f32[4]{0:T(128)} %bitcast.2) | data formatting | bytes 32
  94.8 1.4 %copy.14 = bf16[4,4096]{1,0:T(4,128)(2,1)} copy(bf16[4,4096]{1,0:T(4,128)(2,1)} %get-tuple-element.18) | data formatting | bytes 65536
  96.2 1.5 %copy.15 = f32[16,1024]{1,0:T(8,128)} copy(f32[16,1024]{1,0:T(8,128)} %get-tuple-element.19) | data formatting | bytes 131072

commit v2 on v0

v2 whole, which is shorter than its diff:
```python
import jax
import jax.numpy as jnp
from jax import lax
from jax.experimental import pallas as pl
from jax.experimental.pallas import tpu as pltpu
from jax.sharding import PartitionSpec as P

NY, NZ, NX = 4, 8, 4
PLANE = NY * NX
OWN = 4
SETS = 2
PART = OWN // SETS
H, E = 4096, 1024
BANK = 1024
BLOCK = NZ * PART
SET = PLANE * BLOCK
ROWS = SETS * SET
LANES = 128
SPLIT = E // LANES
TILE = 512
W_PARTS = 8
QUERIES = 1024
MESH = pl.DeviceIdType.MESH
NT = (((1,), (1,)), ((), ()))
POS, STATES = 0, 1
QUERY, STATS, GRAD, PROJ = (2, 3), (4, 5), (6, 7), (8, 9)
STAGES = 10
F32, BF16 = jnp.float32, jnp.bfloat16


def kernel(
    states_ref, w_hbm, bank_hbm, pos_ref,
    loss_ref, top_ref, gs_ref, gw_ref,
    w, bank, posz, posp, stz_out, stz_in, stp_out, slab, slab_t, turn,
    zq, zf, unit_s, radius_s, qall, expo, coef, sp, sz, final, gout, gin,
    gz_out, gz_in, zg, own_gp, gpall, gw_acc, gw_in, lossbuf,
    w_sem, bank_sem, cs, cr, zs, zr, ps, pr,
):
    me = lax.axis_index("dev")
    c = lax.rem(me, 2)
    x = lax.rem(me // 2, NX)
    z = lax.rem(me // (2 * NX), NZ)
    y = me // (2 * NX * NZ)
    p = y * NX + x
    chip = me // 2
    partner = chip * 2 + (1 - c)

    def dev(yy, zz, xx):
        return ((yy * NZ + zz) * NX + xx) * 2 + c

    def rows(i, n, base=0):
        return pl.ds(pl.multiple_of(base + i * n, n), n)

    def slots(ref, n, base=0):
        return lambda s: ref.at[rows(s, n, base), :]

    def copy(src, dst, send_sem, recv_sem, target):
        return pltpu.make_async_remote_copy(
            src_ref=src, dst_ref=dst, send_sem=send_sem, recv_sem=recv_sem,
            device_id=(target,), device_id_type=MESH,
        )

    def z_each(body):
        def step(k, carry):
            body(lax.rem(z + k, NZ))
            return carry
        lax.fori_loop(1, NZ, step, 0)

    def p_each(body):
        def step(k, carry):
            body(lax.rem(y + k // NX, NY) * NX + lax.rem(x + lax.rem(k, NX), NX))
            return carry
        lax.fori_loop(1, PLANE, step, 0)

    z_dev = lambda t: dev(y, t, x)
    p_dev = lambda t: dev(t // NX, z, lax.rem(t, NX))

    def z_send(stage, src, dst):
        z_each(lambda t: copy(src(t), dst(z), zs.at[stage], zr.at[stage], z_dev(t)).start())

    def p_send(stage, src, dst):
        p_each(lambda t: copy(src(t), dst(p), ps.at[stage], pr.at[stage], p_dev(t)).start())

    def z_recv(stage, ref, n, base=0):
        part = ref.at[pl.ds(base, (NZ - 1) * n), :]
        copy(part, part, zs.at[stage], zr.at[stage], partner).wait_recv()

    def z_drain(stage, ref, n):
        part = ref.at[pl.ds(0, (NZ - 1) * n), :]
        copy(part, part, zs.at[stage], zr.at[stage], partner).wait_send()

    def p_recv(stage, ref, n, base=0):
        part = ref.at[pl.ds(base, (PLANE - 1) * n), :]
        copy(part, part, ps.at[stage], pr.at[stage], partner).wait_recv()

    def p_drain(stage, ref, n):
        part = ref.at[pl.ds(0, (PLANE - 1) * n), :]
        copy(part, part, ps.at[stage], pr.at[stage], partner).wait_send()

    def w_copy(i):
        part = pl.ds(i * (H // W_PARTS), H // W_PARTS)
        return pltpu.make_async_copy(w_hbm.at[part, :], w.at[part, :], w_sem.at[i])

    for i in range(W_PARTS):
        w_copy(i).start()
    mine = rows(c, BANK)
    other = rows(1 - c, BANK)
    own_bank = pltpu.make_async_copy(bank_hbm, bank.at[mine, :], bank_sem)
    own_bank.start()

    barrier = pltpu.get_barrier_semaphore()

    def greet(target):
        pl.semaphore_signal(barrier, inc=1, device_id=(target,), device_id_type=MESH)

    greet(partner)
    z_each(lambda t: greet(z_dev(t)))
    p_each(lambda t: greet(p_dev(t)))
    lane = lax.broadcasted_iota(jnp.int32, (8, LANES), 1)
    sub = lax.broadcasted_iota(jnp.int32, (8, LANES), 0)
    own_lane = lax.rem(p, 8) * BLOCK + z
    tile = jnp.zeros((8, LANES), jnp.int32)
    for r in range(OWN):
        at_row, at_lane = (r // PART) * 2 + p // 8, own_lane + (r % PART) * NZ
        tile = jnp.where((lane == at_lane) & (sub == at_row), pos_ref[r], tile)
    posz[rows(z, 8), :] = tile
    states_f = states_ref[...].astype(F32)
    for zz in range(NZ):
        for yy in range(NY):
            at = (yy * NZ + zz) * LANES
            stz_out[pl.ds(zz * 16 + yy, OWN, stride=NY), :] = states_f[:, at:at + LANES]
    stz_in[rows(z, 16), :] = stz_out[rows(z, 16), :]
    pl.semaphore_wait(barrier, 1 + (NZ - 1) + (PLANE - 1))

    bank_out = copy(bank_hbm, bank.at[mine, :], cs.at[0], cr.at[0], partner)
    bank_out.start()

    z_send(POS, lambda t: slots(posz, 8)(z), slots(posz, 8))
    z_send(STATES, slots(stz_out, 16), slots(stz_in, 16))

    proj = jnp.zeros((OWN, E), F32)
    for i in range(W_PARTS):
        w_copy(i).wait()
        part = slice(i * (H // W_PARTS), (i + 1) * (H // W_PARTS))
        proj = proj + jnp.dot(states_ref[:, part], w[part, :], preferred_element_type=F32)
    radius = jnp.sqrt(jnp.sum(proj * proj, axis=1, keepdims=True) + 1e-06)
    unit = proj / radius
    radius_b = jnp.broadcast_to(radius, (OWN, LANES))
    for e in range(SPLIT):
        unit_s[pl.ds(e, OWN, stride=SPLIT), :] = unit[:, e * LANES:(e + 1) * LANES]
        radius_s[pl.ds(e, OWN, stride=SPLIT), :] = radius_b
    zq[rows(z, OWN * SPLIT), :] = unit_s[...].astype(BF16)
    zq_at = slots(zq, OWN * SPLIT)
    z_send(QUERY[0], lambda t: zq_at(z), zq_at)

    z_recv(POS, posz, 8)
    tile = jnp.zeros((8, LANES), jnp.int32)
    for s in range(NZ):
        tile = tile + posz[s * 8:(s + 1) * 8, :]
    posp[rows(p, 8), :] = tile
    p_send(POS, lambda t: slots(posp, 8)(p), slots(posp, 8))
    z_recv(STATES, stz_in, 16)
    for yy in range(NY):
        column_slab = [stz_in[pl.ds(r * NY + yy, NZ, stride=16), :] for r in range(OWN)]
        stp_out[yy * 32:(yy + 1) * 32, :] = jnp.concatenate(column_slab, axis=0).astype(BF16)
    slab[rows(p, 32), :] = stp_out[rows(y, 32), :]

    z_recv(QUERY[0], zq, OWN * SPLIT)

    def assemble(base, step, target, s):
        for e in range(SPLIT):
            block = [zf[pl.ds(base + r * SPLIT + e, NZ, stride=step), :] for r in range(PART)]
            target[rows(p, BLOCK, s * SET), e * LANES:(e + 1) * LANES] = jnp.concatenate(block, axis=0).astype(BF16)

    zf[...] = zq[...].astype(F32)
    for s in range(SETS):
        assemble(s * PART * SPLIT, OWN * SPLIT, qall, s)
        at = slots(qall, BLOCK, s * SET)
        p_send(QUERY[s], lambda t: at(p), at)
    p_send(STATES, lambda t: slots(stp_out, 32)(t // NX), slots(slab, 32))
    own_bank.wait()
    copy(bank.at[other, :], bank.at[other, :], cs.at[0], cr.at[0], partner).wait_recv()
    p_recv(POS, posp, 8)
    tile = jnp.zeros((8, LANES), jnp.int32)
    for s in range(PLANE):
        tile = tile + posp[s * 8:(s + 1) * 8, :]
    final[0:8, :] = (tile - chip * (2 * BANK)).astype(F32)

    eye = lax.broadcasted_iota(jnp.int32, (LANES, LANES), 0) == lax.broadcasted_iota(jnp.int32, (LANES, LANES), 1)
    to_row = lambda col: jnp.sum(jnp.where(eye, jnp.broadcast_to(col, (LANES, LANES)), 0.0), axis=0, keepdims=True)
    to_col = lambda row: jnp.sum(jnp.where(eye, jnp.broadcast_to(row, (LANES, LANES)), 0.0), axis=1, keepdims=True)
    tiles = 2 * BANK // TILE
    column = lax.broadcasted_iota(jnp.int32, (LANES, TILE), 1)

    def scores_of(s):
        mine = pl.multiple_of((s * PLANE + p) * 8, 8)
        sp[pl.ds(mine, 8), :] = jnp.zeros((8, LANES), F32)
        p_recv(QUERY[s], qall, BLOCK, s * SET)

        def half(h, carry):
            at = rows(h, LANES, s * SET)
            hit_col = to_col(final[pl.ds(s * 2 + h, 1), :]).astype(jnp.int32)
            top = jnp.full((LANES, 1), -jnp.inf, F32)
            positive = jnp.zeros((1, LANES), F32)
            for j in range(tiles):
                here = slice(j * TILE, (j + 1) * TILE)
                scores = 20.0 * lax.dot_general(qall[at, :], bank[here, :], NT, preferred_element_type=F32)
                expo[at, here] = scores
                top = jnp.maximum(top, jnp.max(scores, axis=1, keepdims=True))
                found = jnp.sum(jnp.where(column == hit_col - j * TILE, scores, 0.0), axis=0, keepdims=True)
                for g in range(TILE // LANES):
                    positive = positive + found[:, g * LANES:(g + 1) * LANES]
            total = jnp.zeros((LANES, 1), F32)
            for j in range(tiles):
                here = slice(j * TILE, (j + 1) * TILE)
                value = jnp.exp(expo[at, here] - top)
                expo[at, here] = value
                total = total + jnp.sum(value, axis=1, keepdims=True)
            sp[pl.ds(mine + h, 1), :] = to_row(top)
            sp[pl.ds(mine + 2 + h, 1), :] = to_row(total)
            sp[pl.ds(mine + 4, 1), :] += positive
            return carry

        lax.fori_loop(0, 2, half, 0)
        final[8 + s * 8:16 + s * 8, :] = sp[pl.ds(mine, 8), :]
        at = slots(sp, 8, s * PLANE * 8)
        p_send(STATS[s], lambda t: at(p), at)

    def combine(ref, base, n):
        high = ref[base:base + 8, :]
        found = high
        for i in range(1, n):
            part = ref[base + i * 8:base + i * 8 + 8, :]
            high = jnp.maximum(high, part)
            found = found + part
        total = jnp.zeros((2, LANES), F32)
        for i in range(n):
            total = total + ref[base + i * 8 + 2:base + i * 8 + 4, :] * jnp.exp(
                ref[base + i * 8:base + i * 8 + 2, :] - high[0:2, :]
            )
        return high[0:2, :], total, found[4:5, :]

    def plane_stats(s):
        p_recv(STATS[s], sp, 8, s * PLANE * 8)
        high, total, found = combine(sp, s * PLANE * 8, PLANE)
        at = pl.multiple_of((s * NZ + z) * 8, 8)
        sz[pl.ds(at, 2), :] = high
        sz[pl.ds(at + 2, 2), :] = total
        sz[pl.ds(at + 4, 4), :] = jnp.concatenate([found, jnp.zeros((3, LANES), F32)], axis=0)
        there = slots(sz, 8, s * NZ * 8)
        z_send(STATS[s], lambda t: there(z), there)

    def all_stats(s):
        z_recv(STATS[s], sz, 8, s * NZ * 8)
        high, total, found = combine(sz, s * NZ * 8, NZ)
        lse = high + jnp.log(total)
        here = 8 + s * 8
        final[here + 2:here + 4, :] = jnp.exp(final[here:here + 2, :] - lse)
        final[here + 4:here + 6, :] = high
        return jnp.sum(lse, axis=0, keepdims=True) - found

    def grad_of(s):
        def half(h, carry):
            at = rows(h, LANES, s * SET)
            hit_col = to_col(final[pl.ds(s * 2 + h, 1), :]).astype(jnp.int32)
            scale_col = to_col(final[pl.ds(8 + s * 8 + 2 + h, 1), :])
            for j in range(tiles):
                here = slice(j * TILE, (j + 1) * TILE)
                hits = (column == hit_col - j * TILE).astype(F32)
                coef[rows(h, LANES), here] = ((expo[at, here] * scale_col - hits) * (1.0 / QUERIES)).astype(BF16)
            return carry

        lax.fori_loop(0, 2, half, 0)
        for j in range(E // TILE):
            here = slice(j * TILE, (j + 1) * TILE)
            value = 20.0 * jnp.dot(coef[...], bank[:, here], preferred_element_type=F32)
            gout[s * SET:(s + 1) * SET, here] = value.astype(BF16)
        p_send(GRAD[s], slots(gout, BLOCK, s * SET), slots(gin, BLOCK, s * SET))
        gin[rows(p, BLOCK, s * SET), :] = gout[rows(p, BLOCK, s * SET), :]

    scores_of(0)
    scores_of(1)
    plane_stats(0)
    plane_stats(1)
    lost = all_stats(0)
    grad_of(0)
    lost = lost + all_stats(1)
    grad_of(1)
    lossbuf[0:8, :] = jnp.broadcast_to(jnp.sum(lost), (8, LANES))
    loss_out = copy(lossbuf.at[0:8, :], lossbuf.at[8:16, :], cs.at[1], cr.at[1], partner)
    loss_out.start()

    top_tile = jnp.zeros((8, LANES), F32)
    for r in range(OWN):
        row = final[pl.ds(8 + (r // PART) * 8 + 4 + p // 8, 1), :]
        mask = lax.broadcasted_iota(jnp.int32, (1, LANES), 1) == own_lane + (r % PART) * NZ
        value = jnp.sum(jnp.where(mask, row, 0.0))
        top_tile = jnp.where(lane == r, value, top_tile)
    top_ref[...] = top_tile
    p_recv(STATES, slab, 32)
    for s in range(SETS):
        part = slab[...].astype(F32).reshape(PLANE, 32, LANES)[:, s * BLOCK:(s + 1) * BLOCK, :].reshape(SET, LANES)
        turn[...] = jnp.transpose(part)
        slab_t[s] = turn[rows(x, 32), :].astype(BF16)

    def line_grad(s):
        p_recv(GRAD[s], gin, BLOCK, s * SET)

        def add(i, acc):
            return acc + gin[rows(i, BLOCK, s * SET), :].astype(F32)

        acc = lax.fori_loop(0, PLANE, add, jnp.zeros((BLOCK, E), F32))
        base = s * NZ * PART * SPLIT
        for e in range(SPLIT):
            for r in range(PART):
                gz_out[pl.ds(base + r * SPLIT + e, NZ, stride=PART * SPLIT), :] = (
                    acc[r * NZ:(r + 1) * NZ, e * LANES:(e + 1) * LANES])
        here, there = slots(gz_out, 16, base), slots(gz_in, 16, base)
        z_send(GRAD[s], here, there)
        gz_in[rows(z, 16, base), :] = gz_out[rows(z, 16, base), :]

    def own_grad(s):
        base = s * NZ * 16
        z_recv(GRAD[s], gz_in, 16, base)
        grad = gz_in[base:base + 16, :]
        for i in range(1, NZ):
            grad = grad + gz_in[base + i * 16:base + (i + 1) * 16, :]
        for r in range(PART):
            one = slice(s * 16 + r * SPLIT, s * 16 + (r + 1) * SPLIT)
            g, u = grad[r * SPLIT:(r + 1) * SPLIT, :], unit_s[one, :]
            inner = jnp.sum(jnp.sum(u * g, axis=1, keepdims=True), axis=0, keepdims=True)
            own_gp[one, :] = (g - u * inner) / radius_s[one, :]
        zg[rows(z, 16, base), :] = own_gp[s * 16:(s + 1) * 16, :].astype(BF16)
        at = slots(zg, 16, base)
        z_send(PROJ[s], lambda t: at(z), at)

    def share_grad(s):
        base = s * NZ * 16
        z_recv(PROJ[s], zg, 16, base)
        zf[0:NZ * 16, :] = zg[base:base + NZ * 16, :].astype(F32)
        assemble(0, 16, gpall, s)
        at = slots(gpall, BLOCK, s * SET)
        p_send(PROJ[s], lambda t: at(p), at)

    line_grad(0)
    line_grad(1)
    own_grad(0)
    own_grad(1)
    share_grad(0)
    share_grad(1)

    gp = jnp.concatenate(
        [own_gp[pl.ds(e, OWN, stride=SPLIT), :] for e in range(SPLIT)], axis=1
    ).astype(BF16)
    for j in range(H // TILE):
        here = slice(j * TILE, (j + 1) * TILE)
        gs_ref[:, here] = lax.dot_general(gp, w[here, :], NT, preferred_element_type=F32).astype(BF16)

    z_drain(POS, posz, 8)
    z_drain(STATES, stz_out, 16)
    z_drain(QUERY[0], zq, OWN * SPLIT)
    p_drain(POS, posp, 8)
    p_drain(STATES, slab, 32)
    for s in range(SETS):
        z_drain(STATS[s], sz, 8)
        z_drain(GRAD[s], gz_out, 16)
        z_drain(PROJ[s], zg, 16)
        p_drain(QUERY[s], qall, BLOCK)
        p_drain(STATS[s], sp, 8)
        p_drain(GRAD[s], gout, BLOCK)
    bank_out.wait_send()
    loss_out.wait()
    loss_ref[...] = (lossbuf[0:8, :] + lossbuf[8:16, :]) * (1.0 / QUERIES)

    p_recv(PROJ[0], gpall, BLOCK, 0)
    gw_acc[...] = jnp.dot(slab_t[0], gpall[0:SET, :], preferred_element_type=F32)
    p_recv(PROJ[1], gpall, BLOCK, SET)
    gw_acc[...] += jnp.dot(slab_t[1], gpall[SET:ROWS, :], preferred_element_type=F32)
    gw_out = copy(gw_acc.at[rows(1 - c, 16), :], gw_in, cs.at[2], cr.at[2], partner)
    gw_out.start()
    p_drain(PROJ[0], gpall, BLOCK)
    p_drain(PROJ[1], gpall, BLOCK)
    gw_out.wait()
    gw_ref[...] = gw_acc[rows(c, 16), :] + gw_in[...]


def hand_over(loss_in, top_in, gs_in, gw_in, loss_ref, top_ref, gs_ref, gw_ref):
    loss_ref[...] = loss_in[0:1, 0:1]
    top_ref[...] = top_in[0:1, 0:OWN]
    gs_ref[...] = gs_in[...]
    gw_ref[...] = gw_in[...]


def local(states, head_weight, bank, positive_index):
    vmem = pltpu.VMEM
    dma = pltpu.SemaphoreType.DMA
    in_vmem = pl.BlockSpec(memory_space=pltpu.VMEM)
    grads = (jax.ShapeDtypeStruct((OWN, H), BF16), jax.ShapeDtypeStruct((16, E), F32))
    parts = pl.pallas_call(
        kernel,
        out_shape=(jax.ShapeDtypeStruct((8, LANES), F32),) * 2 + grads,
        in_specs=[
            in_vmem,
            pl.BlockSpec(memory_space=pl.ANY),
            pl.BlockSpec(memory_space=pl.ANY),
            pl.BlockSpec(memory_space=pltpu.SMEM),
        ],
        out_specs=(in_vmem,) * 4,
        scratch_shapes=[
            vmem((H, E), BF16),
            vmem((2 * BANK, E), BF16),
            vmem((NZ * 8, LANES), jnp.int32),
            vmem((PLANE * 8, LANES), jnp.int32),
            vmem((NZ * 16, LANES), F32),
            vmem((NZ * 16, LANES), F32),
            vmem((NY * 32, LANES), BF16),
            vmem((ROWS, LANES), BF16),
            vmem((SETS, 32, SET), BF16),
            vmem((LANES, SET), F32),
            vmem((NZ * OWN * SPLIT, LANES), BF16),
            vmem((NZ * OWN * SPLIT, LANES), F32),
            vmem((OWN * SPLIT, LANES), F32),
            vmem((OWN * SPLIT, LANES), F32),
            vmem((ROWS, E), BF16),
            vmem((ROWS, 2 * BANK), F32),
            vmem((SET, 2 * BANK), BF16),
            vmem((SETS * PLANE * 8, LANES), F32),
            vmem((SETS * NZ * 8, LANES), F32),
            vmem((24, LANES), F32),
            vmem((ROWS, E), BF16),
            vmem((ROWS, E), BF16),
            vmem((SETS * NZ * 16, LANES), F32),
            vmem((SETS * NZ * 16, LANES), F32),
            vmem((SETS * NZ * 16, LANES), BF16),
            vmem((OWN * SPLIT, LANES), F32),
            vmem((ROWS, E), BF16),
            vmem((32, E), F32),
            vmem((16, E), F32),
            vmem((16, LANES), F32),
            dma((W_PARTS,)), dma,
            dma((3,)), dma((3,)),
            dma((STAGES,)), dma((STAGES,)),
            dma((STAGES,)), dma((STAGES,)),
        ],
        compiler_params=pltpu.CompilerParams(
            collective_id=0, has_side_effects=True, vmem_limit_bytes=56 * 2**20
        ),
        name="info_nce",
    )(states, head_weight, bank, positive_index)
    loss, top, grad_states, grad_weight = pl.pallas_call(
        hand_over,
        out_shape=(jax.ShapeDtypeStruct((1, 1), F32), jax.ShapeDtypeStruct((1, OWN), F32)) + grads,
        in_specs=[in_vmem] * 4,
        out_specs=(in_vmem,) * 4,
        name="hand_over",
    )(*parts)
    return (loss.reshape(()), top.reshape((OWN,)), grad_states, grad_weight)


def solution(mesh):
    placed = (P("dev", None), P(), P("dev", None), P("dev"))
    return jax.shard_map(
        local,
        mesh=mesh,
        in_specs=placed,
        out_specs=(P(), P("dev"), P("dev", None), P("dev", None)),
        check_vma=False,
    )
```

time: 1890 us -> 79.7 us (0.04)
  waiting for transfers between devices: 1570 us -> 0 us
  blocking collectives: 231 us -> 0 us
  Pallas kernels: 0 us -> 78.8 us
  matrix products: 32.7 us -> 0 us
  local copies, waits for them, and re-layouts: 27.6 us -> 0 us
    unnamed x5 -> x0, waiting for transfers between devices: 1540 us -> none
    unnamed x1 -> x0, blocking collectives: 81.9 us -> none
    pallas_call x0 -> x2, Pallas kernels: none -> 78.8 us  [the longest x1 77.3 us: local(): pl.pallas_call(kernel, out_shape=(jax.ShapeDtypeStruct((8, LANES), F32),)...]
    pmax x1 -> x0, blocking collectives: 76.7 us -> none  [local(): top_score = lax.pmax(local_top, 'dev')]
    psum x1 -> x0, blocking collectives: 72.7 us -> none  [local(): total, positive = lax.psum((local_total, positive_part), 'dev')]
    dot_general x5 -> x0, matrix products: 32.7 us -> none  [the longest x1 8.93 us: local(): lax.dot_general(states, grad_projected, (((0,), (0,)), ((), ())), preferr...]
    all_gather x1 -> x0, waiting for transfers between devices: 26.2 us -> none  [local(): lax.all_gather(query, 'dev', axis=0, tiled=True)]
    unnamed x10 -> x0, local copies, waits for them, and re-layouts: 21.7 us -> none
  transfers between devices with their start and end apart: 3 -> 0, of which waited for: 3 -> 0; matrix products, arithmetic and copies ran while one was open for 0% -> 0% of each run, Pallas kernels for 0% -> 0%
where the time goes in v2:
time: 79.7 us; the launch traced here: 79.5 us
  Pallas kernels  78.8 us (99%)
    pallas_call x1, Pallas kernels, local(): pl.pallas_call(kernel, out_shape=(jax.ShapeDtypeStruct((8, LANES), F32),)...  77.3 us

profile of v2, /device:TPU:1, one launch (start us, length us, event | category | flops | bytes accessed | tf_op | source)
XLA Modules:
  0.0 79.5 jit_solution(17792991217185927056)
XLA Ops:
  0.6 77.3 %info_nce.1 = (f32[8,128]{1,0:T(8,128)}, f32[8,128]{1,0:T(8,128)}, bf16[4,4096]{1,0:T(4,128)(2,1)}, f32[16,1024]{1,0:T(8,128)}) custom-call(bf16[4,4096]{1,0:T(4,128)(2,1)} %states_ref.1, bf16[4096,1024]{1,0:T(8,128)(2,1)} %w_hbm.1, bf16[1024,1024]{1,0:T(8,128)(2,1)} %bank_hbm.1, s32[4]{0:T(128)} %pos_ref.1), custom_call_target="tpu_custom_call" | custom-call | tf_op jit(solution)/shard_map/info_nce/pallas_call | solution.py:399
  78.0 1.5 %hand_over.1 = (f32[1,1]{1,0:T(1,128)}, f32[1,4]{1,0:T(1,128)}, bf16[4,4096]{1,0:T(4,128)(2,1)}, f32[16,1024]{1,0:T(8,128)}) custom-call(f32[8,128]{1,0:T(8,128)} %get-tuple-element.12.loss_in, f32[8,128]{1,0:T(8,128)} %get-tuple-element.13.top_in, bf16[4,4096]{1,0:T(4,128)(2,1)} %get-tuple-element.14.gs_in, f32[16,1024]{1,0:T(8,128)} %get-tuple-element.15.gw_in), custom_call_target="tpu_custom_call" | custom-call | tf_op jit(solution)/shard_map/hand_over/pallas_call | solution.py:450

commit v3 on v2

--- a/solution.py
+++ b/solution.py
@@ -24,7 +24,9 @@
 NT = (((1,), (1,)), ((), ()))
 POS, STATES = 0, 1
 QUERY, STATS, GRAD, PROJ = (2, 3), (4, 5), (6, 7), (8, 9)
-STAGES = 10
+LEFT_X, LEFT_Y, RIGHT_Y, RIGHT_X = (2, 3), (10, 11), (12, 13), (14, 15)
+STAGES = 16
+HALF = E // 2
 F32, BF16 = jnp.float32, jnp.bfloat16
 
 
@@ -32,7 +34,7 @@
     states_ref, w_hbm, bank_hbm, pos_ref,
     loss_ref, top_ref, gs_ref, gw_ref,
     w, bank, posz, posp, stz_out, stz_in, stp_out, slab, slab_t, turn,
-    zq, zf, unit_s, radius_s, qall, expo, coef, sp, sz, final, gout, gin,
+    zq, zf, unit_s, radius_s, qleft, qright, expo, coef, sp, sz, final, gout, gin,
     gz_out, gz_in, zg, own_gp, gpall, gw_acc, gw_in, lossbuf,
     w_sem, bank_sem, cs, cr, zs, zr, ps, pr,
 ):
@@ -62,15 +64,18 @@
 
     def z_each(body):
         def step(k, carry):
-            body(lax.rem(z + k, NZ))
+            body(lax.rem(z + 4 + (k // 2 + k % 2) * (1 - 2 * (k % 2)), NZ))
             return carry
-        lax.fori_loop(1, NZ, step, 0)
+        lax.fori_loop(0, NZ - 1, step, 0)
+
+    def away(k):
+        return 2 * (1 - k % 2) + (k % 2 + k // 2) % 2
 
     def p_each(body):
         def step(k, carry):
-            body(lax.rem(y + k // NX, NY) * NX + lax.rem(x + lax.rem(k, NX), NX))
+            body(lax.rem(y + away(k // NX), NY) * NX + lax.rem(x + away(k % NX), NX))
             return carry
-        lax.fori_loop(1, PLANE, step, 0)
+        lax.fori_loop(0, PLANE - 1, step, 0)
 
     z_dev = lambda t: dev(y, t, x)
     p_dev = lambda t: dev(t // NX, z, lax.rem(t, NX))
@@ -106,7 +111,6 @@
     mine = rows(c, BANK)
     other = rows(1 - c, BANK)
     own_bank = pltpu.make_async_copy(bank_hbm, bank.at[mine, :], bank_sem)
-    own_bank.start()
 
     barrier = pltpu.get_barrier_semaphore()
 
@@ -133,10 +137,11 @@
     pl.semaphore_wait(barrier, 1 + (NZ - 1) + (PLANE - 1))
 
     bank_out = copy(bank_hbm, bank.at[mine, :], cs.at[0], cr.at[0], partner)
-    bank_out.start()
-
     z_send(POS, lambda t: slots(posz, 8)(z), slots(posz, 8))
     z_send(STATES, slots(stz_out, 16), slots(stz_in, 16))
+
+    bank_out.start()
+    own_bank.start()
 
     proj = jnp.zeros((OWN, E), F32)
     for i in range(W_PARTS):
@@ -167,16 +172,38 @@
 
     z_recv(QUERY[0], zq, OWN * SPLIT)
 
-    def assemble(base, step, target, s):
-        for e in range(SPLIT):
-            block = [zf[pl.ds(base + r * SPLIT + e, NZ, stride=step), :] for r in range(PART)]
-            target[rows(p, BLOCK, s * SET), e * LANES:(e + 1) * LANES] = jnp.concatenate(block, axis=0).astype(BF16)
+    def gathered(base, step, e):
+        block = [zf[pl.ds(base + r * SPLIT + e, NZ, stride=step), :] for r in range(PART)]
+        return jnp.concatenate(block, axis=0).astype(BF16)
+
+    x_peers = [lax.rem(x + k, NX) for k in (2, 1, 3)]
+    y_peers = [lax.rem(y + k, NY) for k in (2, 1, 3)]
+
+    def p_start(stage, ref, target):
+        copy(ref, ref, ps.at[stage], pr.at[stage], target).start()
 
     zf[...] = zq[...].astype(F32)
     for s in range(SETS):
-        assemble(s * PART * SPLIT, OWN * SPLIT, qall, s)
-        at = slots(qall, BLOCK, s * SET)
-        p_send(QUERY[s], lambda t: at(p), at)
+        for e in range(SPLIT // 2):
+            here = slice(e * LANES, (e + 1) * LANES)
+            qleft[s * NY + y, x, :, here] = gathered(s * PART * SPLIT, OWN * SPLIT, e)
+            qright[s * NY + y, x, :, here] = gathered(s * PART * SPLIT, OWN * SPLIT, SPLIT // 2 + e)
+        for i in range(3):
+            p_start(LEFT_X[s], qleft.at[s * NY + y, x], dev(y, z, x_peers[i]))
+            p_start(RIGHT_Y[s], qright.at[s * NY + y, x], dev(y_peers[i], z, x))
+
+    def q_wait(stage, ref):
+        return copy(ref, ref, ps.at[stage], pr.at[stage], partner)
+
+    three_blocks = lambda ref, s: ref.at[s * NY, pl.ds(0, 3)]
+    three_lines = lambda ref, s: ref.at[pl.ds(s * NY, 3)]
+    for s in range(SETS):
+        q_wait(LEFT_X[s], three_blocks(qleft, s)).wait_recv()
+        for i in range(3):
+            p_start(LEFT_Y[s], qleft.at[s * NY + y], dev(y_peers[i], z, x))
+        q_wait(RIGHT_Y[s], three_blocks(qright, s)).wait_recv()
+        for i in range(3):
+            p_start(RIGHT_X[s], qright.at[pl.ds(s * NY, NY), x], dev(y, z, x_peers[i]))
     p_send(STATES, lambda t: slots(stp_out, 32)(t // NX), slots(slab, 32))
     own_bank.wait()
     copy(bank.at[other, :], bank.at[other, :], cs.at[0], cr.at[0], partner).wait_recv()
@@ -190,38 +217,46 @@
     to_row = lambda col: jnp.sum(jnp.where(eye, jnp.broadcast_to(col, (LANES, LANES)), 0.0), axis=0, keepdims=True)
     to_col = lambda row: jnp.sum(jnp.where(eye, jnp.broadcast_to(row, (LANES, LANES)), 0.0), axis=1, keepdims=True)
     tiles = 2 * BANK // TILE
-    column = lax.broadcasted_iota(jnp.int32, (LANES, TILE), 1)
+    column = lax.broadcasted_iota(jnp.int32, (SET, LANES), 1)
+    two_cols = lambda base: jnp.concatenate([to_col(final[base + h:base + h + 1, :]) for h in range(2)], axis=0)
+    hits_of = lambda s: two_cols(s * 2).astype(jnp.int32)
 
     def scores_of(s):
         mine = pl.multiple_of((s * PLANE + p) * 8, 8)
         sp[pl.ds(mine, 8), :] = jnp.zeros((8, LANES), F32)
-        p_recv(QUERY[s], qall, BLOCK, s * SET)
-
-        def half(h, carry):
-            at = rows(h, LANES, s * SET)
-            hit_col = to_col(final[pl.ds(s * 2 + h, 1), :]).astype(jnp.int32)
-            top = jnp.full((LANES, 1), -jnp.inf, F32)
-            positive = jnp.zeros((1, LANES), F32)
-            for j in range(tiles):
-                here = slice(j * TILE, (j + 1) * TILE)
-                scores = 20.0 * lax.dot_general(qall[at, :], bank[here, :], NT, preferred_element_type=F32)
-                expo[at, here] = scores
-                top = jnp.maximum(top, jnp.max(scores, axis=1, keepdims=True))
-                found = jnp.sum(jnp.where(column == hit_col - j * TILE, scores, 0.0), axis=0, keepdims=True)
-                for g in range(TILE // LANES):
-                    positive = positive + found[:, g * LANES:(g + 1) * LANES]
-            total = jnp.zeros((LANES, 1), F32)
-            for j in range(tiles):
-                here = slice(j * TILE, (j + 1) * TILE)
-                value = jnp.exp(expo[at, here] - top)
-                expo[at, here] = value
-                total = total + jnp.sum(value, axis=1, keepdims=True)
-            sp[pl.ds(mine + h, 1), :] = to_row(top)
-            sp[pl.ds(mine + 2 + h, 1), :] = to_row(total)
-            sp[pl.ds(mine + 4, 1), :] += positive
-            return carry
-
-        lax.fori_loop(0, 2, half, 0)
+        q_wait(LEFT_Y[s], three_lines(qleft, s)).wait_recv()
+        q_wait(RIGHT_X[s], three_lines(qright, s)).wait_recv()
+        at = slice(s * SET, (s + 1) * SET)
+        left = qleft[s * NY:(s + 1) * NY].reshape(SET, HALF)
+        right = qright[s * NY:(s + 1) * NY].reshape(SET, HALF)
+        hit_col = hits_of(s)
+        groups = [slice(g * LANES, (g + 1) * LANES) for g in range(TILE // LANES)]
+        top, positive = None, jnp.zeros((SET, LANES), F32)
+        for j in range(tiles):
+            here = slice(j * TILE, (j + 1) * TILE)
+            scores = 20.0 * (
+                lax.dot_general(left, bank[here, 0:HALF], NT, preferred_element_type=F32)
+                + lax.dot_general(right, bank[here, HALF:E], NT, preferred_element_type=F32)
+            )
+            expo[at, here] = scores
+            for g in groups:
+                part = scores[:, g]
+                top = part if top is None else jnp.maximum(top, part)
+                positive = positive + jnp.where(column == hit_col - (j * TILE + g.start), part, 0.0)
+        top = jnp.max(top, axis=1, keepdims=True)
+        total = jnp.zeros((SET, LANES), F32)
+        for j in range(tiles):
+            here = slice(j * TILE, (j + 1) * TILE)
+            value = jnp.exp(expo[at, here] - top)
+            expo[at, here] = value
+            for g in groups:
+                total = total + value[:, g]
+        total = jnp.sum(total, axis=1, keepdims=True)
+        for h in range(2):
+            half = slice(h * LANES, (h + 1) * LANES)
+            sp[pl.ds(mine + h, 1), :] = to_row(top[half, :])
+            sp[pl.ds(mine + 2 + h, 1), :] = to_row(total[half, :])
+        sp[pl.ds(mine + 4, 1), :] = jnp.sum(positive, axis=0, keepdims=True)
         final[8 + s * 8:16 + s * 8, :] = sp[pl.ds(mine, 8), :]
         at = slots(sp, 8, s * PLANE * 8)
         p_send(STATS[s], lambda t: at(p), at)
@@ -260,17 +295,13 @@
         return jnp.sum(lse, axis=0, keepdims=True) - found
 
     def grad_of(s):
-        def half(h, carry):
-            at = rows(h, LANES, s * SET)
-            hit_col = to_col(final[pl.ds(s * 2 + h, 1), :]).astype(jnp.int32)
-            scale_col = to_col(final[pl.ds(8 + s * 8 + 2 + h, 1), :])
-            for j in range(tiles):
-                here = slice(j * TILE, (j + 1) * TILE)
-                hits = (column == hit_col - j * TILE).astype(F32)
-                coef[rows(h, LANES), here] = ((expo[at, here] * scale_col - hits) * (1.0 / QUERIES)).astype(BF16)
-            return carry
-
-        lax.fori_loop(0, 2, half, 0)
+        at = slice(s * SET, (s + 1) * SET)
+        hit_col = hits_of(s)
+        scale_col = two_cols(8 + s * 8 + 2)
+        for j in range(2 * BANK // LANES):
+            here = slice(j * LANES, (j + 1) * LANES)
+            hits = (column == hit_col - j * LANES).astype(F32)
+            coef[:, here] = ((expo[at, here] * scale_col - hits) * (1.0 / QUERIES)).astype(BF16)
         for j in range(E // TILE):
             here = slice(j * TILE, (j + 1) * TILE)
             value = 20.0 * jnp.dot(coef[...], bank[:, here], preferred_element_type=F32)
@@ -338,7 +369,8 @@
         base = s * NZ * 16
         z_recv(PROJ[s], zg, 16, base)
         zf[0:NZ * 16, :] = zg[base:base + NZ * 16, :].astype(F32)
-        assemble(0, 16, gpall, s)
+        for e in range(SPLIT):
+            gpall[rows(p, BLOCK, s * SET), e * LANES:(e + 1) * LANES] = gathered(0, 16, e)
         at = slots(gpall, BLOCK, s * SET)
         p_send(PROJ[s], lambda t: at(p), at)
 
@@ -365,7 +397,10 @@
         z_drain(STATS[s], sz, 8)
         z_drain(GRAD[s], gz_out, 16)
         z_drain(PROJ[s], zg, 16)
-        p_drain(QUERY[s], qall, BLOCK)
+        q_wait(LEFT_X[s], three_blocks(qleft, s)).wait_send()
+        q_wait(LEFT_Y[s], three_lines(qleft, s)).wait_send()
+        q_wait(RIGHT_Y[s], three_blocks(qright, s)).wait_send()
+        q_wait(RIGHT_X[s], three_lines(qright, s)).wait_send()
         p_drain(STATS[s], sp, 8)
         p_drain(GRAD[s], gout, BLOCK)
     bank_out.wait_send()
@@ -421,7 +456,8 @@
             vmem((NZ * OWN * SPLIT, LANES), F32),
             vmem((OWN * SPLIT, LANES), F32),
             vmem((OWN * SPLIT, LANES), F32),
-            vmem((ROWS, E), BF16),
+            vmem((SETS * NY, NX, BLOCK, HALF), BF16),
+            vmem((SETS * NY, NX, BLOCK, HALF), BF16),
             vmem((ROWS, 2 * BANK), F32),
             vmem((SET, 2 * BANK), BF16),
             vmem((SETS * PLANE * 8, LANES), F32),

time: 79.7 us -> 70.9 us (0.89)
  Pallas kernels: 78.8 us -> 70.1 us
    pallas_call x1, Pallas kernels: 77.3 us -> 68.6 us  [local(): pl.pallas_call(kernel, out_shape=(jax.ShapeDtypeStruct((8, LANES), F32),)...]
where the time goes in v3:
time: 70.9 us; the launch traced here: 70.7 us
  Pallas kernels  70.1 us (99%)
    pallas_call x1, Pallas kernels, local(): pl.pallas_call(kernel, out_shape=(jax.ShapeDtypeStruct((8, LANES), F32),)...  68.6 us
    pallas_call x1, Pallas kernels, local(): pl.pallas_call(hand_over, out_shape=(jax.ShapeDtypeStruct((1, 1), F32), j...  1.52 us

profile of v3, /device:TPU:1, one launch (start us, length us, event | category | flops | bytes accessed | tf_op | source)
XLA Modules:
  0.0 70.7 jit_solution(13608154856836886465)
XLA Ops:
  0.6 68.6 %info_nce.1 = (f32[8,128]{1,0:T(8,128)}, f32[8,128]{1,0:T(8,128)}, bf16[4,4096]{1,0:T(4,128)(2,1)}, f32[16,1024]{1,0:T(8,128)}) custom-call(bf16[4,4096]{1,0:T(4,128)(2,1)} %states_ref.1, bf16[4096,1024]{1,0:T(8,128)(2,1)} %w_hbm.1, bf16[1024,1024]{1,0:T(8,128)(2,1)} %bank_hbm.1, s32[4]{0:T(128)} %pos_ref.1), custom_call_target="tpu_custom_call" | custom-call | tf_op jit(solution)/shard_map/info_nce/pallas_call | solution.py:434
  69.2 1.5 %hand_over.1 = (f32[1,1]{1,0:T(1,128)}, f32[1,4]{1,0:T(1,128)}, bf16[4,4096]{1,0:T(4,128)(2,1)}, f32[16,1024]{1,0:T(8,128)}) custom-call(f32[8,128]{1,0:T(8,128)} %get-tuple-element.12.loss_in, f32[8,128]{1,0:T(8,128)} %get-tuple-element.13.top_in, bf16[4,4096]{1,0:T(4,128)(2,1)} %get-tuple-element.14.gs_in, f32[16,1024]{1,0:T(8,128)} %get-tuple-element.15.gw_in), custom_call_target="tpu_custom_call" | custom-call | tf_op jit(solution)/shard_map/hand_over/pallas_call | solution.py:486

commit v4 on v3

--- a/solution.py
+++ b/solution.py
@@ -25,6 +25,7 @@
 POS, STATES = 0, 1
 QUERY, STATS, GRAD, PROJ = (2, 3), (4, 5), (6, 7), (8, 9)
 LEFT_X, LEFT_Y, RIGHT_Y, RIGHT_X = (2, 3), (10, 11), (12, 13), (14, 15)
+UNIT, TURNED, OWNERS, WEIGHT = 3, 10, 8, 9
 STAGES = 16
 HALF = E // 2
 F32, BF16 = jnp.float32, jnp.bfloat16
@@ -33,9 +34,9 @@
 def kernel(
     states_ref, w_hbm, bank_hbm, pos_ref,
     loss_ref, top_ref, gs_ref, gw_ref,
-    w, bank, posz, posp, stz_out, stz_in, stp_out, slab, slab_t, turn,
-    zq, zf, unit_s, radius_s, qleft, qright, expo, coef, sp, sz, final, gout, gin,
-    gz_out, gz_in, zg, own_gp, gpall, gw_acc, gw_in, lossbuf,
+    w, bank, posz, posp, stz_out, stz_in, stp_out, slab, turned, turn,
+    zq, zf, unit_s, uz_out, uz_in, qleft, qright, expo, coef, pre, chosen, sp, sz, final, gout, gin,
+    gz_out, gz_in, gs_out, gs_in, gpall, gw_all, gw_in, gw_out, gw_parts, lossbuf,
     w_sem, bank_sem, cs, cr, zs, zr, ps, pr,
 ):
     me = lax.axis_index("dev")
@@ -150,13 +151,17 @@
         proj = proj + jnp.dot(states_ref[:, part], w[part, :], preferred_element_type=F32)
     radius = jnp.sqrt(jnp.sum(proj * proj, axis=1, keepdims=True) + 1e-06)
     unit = proj / radius
-    radius_b = jnp.broadcast_to(radius, (OWN, LANES))
     for e in range(SPLIT):
         unit_s[pl.ds(e, OWN, stride=SPLIT), :] = unit[:, e * LANES:(e + 1) * LANES]
-        radius_s[pl.ds(e, OWN, stride=SPLIT), :] = radius_b
     zq[rows(z, OWN * SPLIT), :] = unit_s[...].astype(BF16)
     zq_at = slots(zq, OWN * SPLIT)
     z_send(QUERY[0], lambda t: zq_at(z), zq_at)
+    radius_b = jnp.broadcast_to(radius, (OWN, LANES))
+    for e in range(SPLIT):
+        uz_out[e * 8:e * 8 + OWN, :] = unit[:, e * LANES:(e + 1) * LANES]
+        uz_out[e * 8 + OWN:(e + 1) * 8, :] = radius_b
+    uz_in[rows(z, 8), :] = uz_out[rows(z, 8), :]
+    z_send(UNIT, slots(uz_out, 8), slots(uz_in, 8))
 
     z_recv(POS, posz, 8)
     tile = jnp.zeros((8, LANES), jnp.int32)
@@ -220,6 +225,18 @@
     column = lax.broadcasted_iota(jnp.int32, (SET, LANES), 1)
     two_cols = lambda base: jnp.concatenate([to_col(final[base + h:base + h + 1, :]) for h in range(2)], axis=0)
     hits_of = lambda s: two_cols(s * 2).astype(jnp.int32)
+
+    def pick(s):
+        hit_col = hits_of(s)
+        for j in range(2 * BANK // LANES):
+            coef[:, j * LANES:(j + 1) * LANES] = (column == hit_col - j * LANES).astype(F32).astype(BF16)
+        for j in range(E // TILE):
+            here = slice(j * TILE, (j + 1) * TILE)
+            chosen[s * SET:(s + 1) * SET, here] = jnp.dot(
+                coef[...], bank[:, here], preferred_element_type=F32).astype(BF16)
+
+    pick(0)
+    pick(1)
 
     def scores_of(s):
         mine = pl.multiple_of((s * PLANE + p) * 8, 8)
@@ -294,29 +311,42 @@
         final[here + 4:here + 6, :] = high
         return jnp.sum(lse, axis=0, keepdims=True) - found
 
-    def grad_of(s):
+    def rough_grad(s):
         at = slice(s * SET, (s + 1) * SET)
         hit_col = hits_of(s)
-        scale_col = two_cols(8 + s * 8 + 2)
+        own = jnp.zeros((SET, LANES), F32)
         for j in range(2 * BANK // LANES):
             here = slice(j * LANES, (j + 1) * LANES)
-            hits = (column == hit_col - j * LANES).astype(F32)
-            coef[:, here] = ((expo[at, here] * scale_col - hits) * (1.0 / QUERIES)).astype(BF16)
+            hit = column == hit_col - j * LANES
+            value = expo[at, here]
+            own = own + jnp.where(hit, value, 0.0)
+            coef[:, here] = jnp.where(hit, 0.0, value).astype(BF16)
         for j in range(E // TILE):
             here = slice(j * TILE, (j + 1) * TILE)
-            value = 20.0 * jnp.dot(coef[...], bank[:, here], preferred_element_type=F32)
-            gout[s * SET:(s + 1) * SET, here] = value.astype(BF16)
+            pre[at, here] = jnp.dot(coef[...], bank[:, here], preferred_element_type=F32)
+        return jnp.sum(own, axis=1, keepdims=True)
+
+    def grad_of(s, own):
+        at = slice(s * SET, (s + 1) * SET)
+        scale_col = two_cols(8 + s * 8 + 2)
+        positive_col = 20.0 * ((own * scale_col - 1.0) * (1.0 / QUERIES)).astype(BF16).astype(F32)
+        scale_col = scale_col * (20.0 / QUERIES)
+        for j in range(SPLIT):
+            here = slice(j * LANES, (j + 1) * LANES)
+            gout[at, here] = (pre[at, here] * scale_col + chosen[at, here].astype(F32) * positive_col).astype(BF16)
         p_send(GRAD[s], slots(gout, BLOCK, s * SET), slots(gin, BLOCK, s * SET))
         gin[rows(p, BLOCK, s * SET), :] = gout[rows(p, BLOCK, s * SET), :]
 
     scores_of(0)
     scores_of(1)
+    own_0 = rough_grad(0)
     plane_stats(0)
+    own_1 = rough_grad(1)
     plane_stats(1)
     lost = all_stats(0)
-    grad_of(0)
+    grad_of(0, own_0)
     lost = lost + all_stats(1)
-    grad_of(1)
+    grad_of(1, own_1)
     lossbuf[0:8, :] = jnp.broadcast_to(jnp.sum(lost), (8, LANES))
     loss_out = copy(lossbuf.at[0:8, :], lossbuf.at[8:16, :], cs.at[1], cr.at[1], partner)
     loss_out.start()
@@ -332,7 +362,8 @@
     for s in range(SETS):
         part = slab[...].astype(F32).reshape(PLANE, 32, LANES)[:, s * BLOCK:(s + 1) * BLOCK, :].reshape(SET, LANES)
         turn[...] = jnp.transpose(part)
-        slab_t[s] = turn[rows(x, 32), :].astype(BF16)
+        turned[rows(z, 32), s * SET:(s + 1) * SET] = turn[rows(x, 32), :].astype(BF16)
+    z_send(TURNED, lambda t: slots(turned, 32)(z), slots(turned, 32))
 
     def line_grad(s):
         p_recv(GRAD[s], gin, BLOCK, s * SET)
@@ -341,62 +372,53 @@
             return acc + gin[rows(i, BLOCK, s * SET), :].astype(F32)
 
         acc = lax.fori_loop(0, PLANE, add, jnp.zeros((BLOCK, E), F32))
-        base = s * NZ * PART * SPLIT
+        query = jnp.concatenate([qleft[s * NY + y, x], qright[s * NY + y, x]], axis=1).astype(F32)
+        inner = jnp.sum(query * acc, axis=1, keepdims=True)
+        inner = jnp.where(lane == 0, inner[0:NZ, :], jnp.where(lane == 1, inner[NZ:2 * NZ, :], 0.0))
+        base = s * NZ * 24
         for e in range(SPLIT):
-            for r in range(PART):
-                gz_out[pl.ds(base + r * SPLIT + e, NZ, stride=PART * SPLIT), :] = (
-                    acc[r * NZ:(r + 1) * NZ, e * LANES:(e + 1) * LANES])
-        here, there = slots(gz_out, 16, base), slots(gz_in, 16, base)
-        z_send(GRAD[s], here, there)
-        gz_in[rows(z, 16, base), :] = gz_out[rows(z, 16, base), :]
-
-    def own_grad(s):
-        base = s * NZ * 16
-        z_recv(GRAD[s], gz_in, 16, base)
-        grad = gz_in[base:base + 16, :]
+            gz_out[base + e * 24:base + e * 24 + BLOCK, :] = acc[:, e * LANES:(e + 1) * LANES]
+            gz_out[base + e * 24 + BLOCK:base + (e + 1) * 24, :] = inner
+        z_send(GRAD[s], slots(gz_out, 24, base), slots(gz_in, 24, base))
+        gz_in[rows(z, 24, base), :] = gz_out[rows(z, 24, base), :]
+
+    def slice_grad(s):
+        base = s * NZ * 24
+        z_recv(GRAD[s], gz_in, 24, base)
+        grad = gz_in[base:base + 24, :]
         for i in range(1, NZ):
-            grad = grad + gz_in[base + i * 16:base + (i + 1) * 16, :]
+            grad = grad + gz_in[base + i * 24:base + (i + 1) * 24, :]
+        block = []
         for r in range(PART):
-            one = slice(s * 16 + r * SPLIT, s * 16 + (r + 1) * SPLIT)
-            g, u = grad[r * SPLIT:(r + 1) * SPLIT, :], unit_s[one, :]
-            inner = jnp.sum(jnp.sum(u * g, axis=1, keepdims=True), axis=0, keepdims=True)
-            own_gp[one, :] = (g - u * inner) / radius_s[one, :]
-        zg[rows(z, 16, base), :] = own_gp[s * 16:(s + 1) * 16, :].astype(BF16)
-        at = slots(zg, 16, base)
-        z_send(PROJ[s], lambda t: at(z), at)
-
-    def share_grad(s):
-        base = s * NZ * 16
-        z_recv(PROJ[s], zg, 16, base)
-        zf[0:NZ * 16, :] = zg[base:base + NZ * 16, :].astype(F32)
-        for e in range(SPLIT):
-            gpall[rows(p, BLOCK, s * SET), e * LANES:(e + 1) * LANES] = gathered(0, 16, e)
+            inner = jnp.sum(jnp.where(lane == r, grad[BLOCK:24, :], 0.0), axis=1, keepdims=True)
+            u = uz_in[pl.ds(s * PART + r, NZ, stride=8), :]
+            radius = uz_in[pl.ds(OWN + s * PART + r, NZ, stride=8), :]
+            block.append((grad[r * NZ:(r + 1) * NZ, :] - u * inner) / radius)
+        rounded = jnp.concatenate(block, axis=0).astype(BF16)
+        gpall[rows(p, BLOCK, s * SET), :] = rounded
         at = slots(gpall, BLOCK, s * SET)
         p_send(PROJ[s], lambda t: at(p), at)
-
+        for r in range(PART):
+            gs_out[pl.ds(s * PART + r, NZ, stride=8), :] = rounded.astype(F32)[r * NZ:(r + 1) * NZ, :]
+
+    gs_out[...] = jnp.zeros_like(gs_out)
     line_grad(0)
     line_grad(1)
-    own_grad(0)
-    own_grad(1)
-    share_grad(0)
-    share_grad(1)
-
-    gp = jnp.concatenate(
-        [own_gp[pl.ds(e, OWN, stride=SPLIT), :] for e in range(SPLIT)], axis=1
-    ).astype(BF16)
-    for j in range(H // TILE):
-        here = slice(j * TILE, (j + 1) * TILE)
-        gs_ref[:, here] = lax.dot_general(gp, w[here, :], NT, preferred_element_type=F32).astype(BF16)
+    z_recv(UNIT, uz_in, 8)
+    slice_grad(0)
+    slice_grad(1)
+    z_send(OWNERS, slots(gs_out, 8), slots(gs_in, 8))
+    gs_in[rows(z, 8), :] = gs_out[rows(z, 8), :]
 
     z_drain(POS, posz, 8)
     z_drain(STATES, stz_out, 16)
     z_drain(QUERY[0], zq, OWN * SPLIT)
+    z_drain(UNIT, uz_out, 8)
     p_drain(POS, posp, 8)
     p_drain(STATES, slab, 32)
     for s in range(SETS):
         z_drain(STATS[s], sz, 8)
-        z_drain(GRAD[s], gz_out, 16)
-        z_drain(PROJ[s], zg, 16)
+        z_drain(GRAD[s], gz_out, 24)
         q_wait(LEFT_X[s], three_blocks(qleft, s)).wait_send()
         q_wait(LEFT_Y[s], three_lines(qleft, s)).wait_send()
         q_wait(RIGHT_Y[s], three_blocks(qright, s)).wait_send()
@@ -407,16 +429,32 @@
     loss_out.wait()
     loss_ref[...] = (lossbuf[0:8, :] + lossbuf[8:16, :]) * (1.0 / QUERIES)
 
+    z_recv(TURNED, turned, 32)
     p_recv(PROJ[0], gpall, BLOCK, 0)
-    gw_acc[...] = jnp.dot(slab_t[0], gpall[0:SET, :], preferred_element_type=F32)
+    weight = jnp.dot(turned[:, 0:SET], gpall[0:SET, :], preferred_element_type=F32)
     p_recv(PROJ[1], gpall, BLOCK, SET)
-    gw_acc[...] += jnp.dot(slab_t[1], gpall[SET:ROWS, :], preferred_element_type=F32)
-    gw_out = copy(gw_acc.at[rows(1 - c, 16), :], gw_in, cs.at[2], cr.at[2], partner)
-    gw_out.start()
+    weight = weight + jnp.dot(turned[:, SET:ROWS], gpall[SET:ROWS, :], preferred_element_type=F32)
+    gw_all[...] = weight.reshape(NZ, 32, LANES)
+    core_out = copy(gw_all.at[:, rows(1 - c, 16), :], gw_in, cs.at[2], cr.at[2], partner)
+    core_out.start()
+    z_drain(TURNED, turned, 32)
     p_drain(PROJ[0], gpall, BLOCK)
     p_drain(PROJ[1], gpall, BLOCK)
-    gw_out.wait()
-    gw_ref[...] = gw_acc[rows(c, 16), :] + gw_in[...]
+    core_out.wait()
+    gw_out[...] = (gw_all[:, rows(c, 16), :] + gw_in[...]).reshape(NZ * 16, LANES)
+    z_send(WEIGHT, slots(gw_out, 16), slots(gw_parts, 16))
+    gw_parts[rows(z, 16), :] = gw_out[rows(z, 16), :]
+
+    z_recv(OWNERS, gs_in, 8)
+    gp = jnp.concatenate([gs_in[e * 8:e * 8 + OWN, :] for e in range(SPLIT)], axis=1).astype(BF16)
+    for j in range(H // TILE):
+        here = slice(j * TILE, (j + 1) * TILE)
+        gs_ref[:, here] = lax.dot_general(gp, w[here, :], NT, preferred_element_type=F32).astype(BF16)
+    z_drain(OWNERS, gs_out, 8)
+    z_recv(WEIGHT, gw_parts, 16)
+    for e in range(SPLIT):
+        gw_ref[:, e * LANES:(e + 1) * LANES] = gw_parts[e * 16:(e + 1) * 16, :]
+    z_drain(WEIGHT, gw_out, 16)
 
 
 def hand_over(loss_in, top_in, gs_in, gw_in, loss_ref, top_ref, gs_ref, gw_ref):
@@ -450,28 +488,33 @@
             vmem((NZ * 16, LANES), F32),
             vmem((NY * 32, LANES), BF16),
             vmem((ROWS, LANES), BF16),
-            vmem((SETS, 32, SET), BF16),
+            vmem((NZ * 32, ROWS), BF16),
             vmem((LANES, SET), F32),
             vmem((NZ * OWN * SPLIT, LANES), BF16),
             vmem((NZ * OWN * SPLIT, LANES), F32),
             vmem((OWN * SPLIT, LANES), F32),
-            vmem((OWN * SPLIT, LANES), F32),
+            vmem((NZ * 8, LANES), F32),
+            vmem((NZ * 8, LANES), F32),
             vmem((SETS * NY, NX, BLOCK, HALF), BF16),
             vmem((SETS * NY, NX, BLOCK, HALF), BF16),
             vmem((ROWS, 2 * BANK), F32),
             vmem((SET, 2 * BANK), BF16),
+            vmem((ROWS, E), F32),
+            vmem((ROWS, E), BF16),
             vmem((SETS * PLANE * 8, LANES), F32),
             vmem((SETS * NZ * 8, LANES), F32),
             vmem((24, LANES), F32),
             vmem((ROWS, E), BF16),
             vmem((ROWS, E), BF16),
-            vmem((SETS * NZ * 16, LANES), F32),
-            vmem((SETS * NZ * 16, LANES), F32),
-            vmem((SETS * NZ * 16, LANES), BF16),
-            vmem((OWN * SPLIT, LANES), F32),
-            vmem((ROWS, E), BF16),
-            vmem((32, E), F32),
-            vmem((16, E), F32),
+            vmem((SETS * NZ * 24, LANES), F32),
+            vmem((SETS * NZ * 24, LANES), F32),
+            vmem((NZ * 8, LANES), F32),
+            vmem((NZ * 8, LANES), F32),
+            vmem((ROWS, LANES), BF16),
+            vmem((NZ, 32, LANES), F32),
+            vmem((NZ, 16, LANES), F32),
+            vmem((NZ * 16, LANES), F32),
+            vmem((NZ * 16, LANES), F32),
             vmem((16, LANES), F32),
             dma((W_PARTS,)), dma,
             dma((3,)), dma((3,)),

time: 70.9 us -> 68.3 us (0.963)
  Pallas kernels: 70.1 us -> 67.4 us
    pallas_call x1, Pallas kernels: 68.6 us -> 65.9 us  [local(): pl.pallas_call(kernel, out_shape=(jax.ShapeDtypeStruct((8, LANES), F32),)...]
where the time goes in v4:
time: 68.3 us; the launch traced here: 68.1 us
  Pallas kernels  67.4 us (99%)
    pallas_call x1, Pallas kernels, local(): pl.pallas_call(kernel, out_shape=(jax.ShapeDtypeStruct((8, LANES), F32),)...  65.9 us
    pallas_call x1, Pallas kernels, local(): pl.pallas_call(hand_over, out_shape=(jax.ShapeDtypeStruct((1, 1), F32), j...  1.52 us

profile of v4, /device:TPU:1, one launch (start us, length us, event | category | flops | bytes accessed | tf_op | source)
XLA Modules:
  0.0 68.1 jit_solution(12334395007671219227)
XLA Ops:
  0.6 65.9 %info_nce.1 = (f32[8,128]{1,0:T(8,128)}, f32[8,128]{1,0:T(8,128)}, bf16[4,4096]{1,0:T(4,128)(2,1)}, f32[16,1024]{1,0:T(8,128)}) custom-call(bf16[4,4096]{1,0:T(4,128)(2,1)} %states_ref.1, bf16[4096,1024]{1,0:T(8,128)(2,1)} %w_hbm.1, bf16[1024,1024]{1,0:T(8,128)(2,1)} %bank_hbm.1, s32[4]{0:T(128)} %pos_ref.1), custom_call_target="tpu_custom_call" | custom-call | tf_op jit(solution)/shard_map/info_nce/pallas_call | solution.py:472
  66.5 1.5 %hand_over.1 = (f32[1,1]{1,0:T(1,128)}, f32[1,4]{1,0:T(1,128)}, bf16[4,4096]{1,0:T(4,128)(2,1)}, f32[16,1024]{1,0:T(8,128)}) custom-call(f32[8,128]{1,0:T(8,128)} %get-tuple-element.12.loss_in, f32[8,128]{1,0:T(8,128)} %get-tuple-element.13.top_in, bf16[4,4096]{1,0:T(4,128)(2,1)} %get-tuple-element.14.gs_in, f32[16,1024]{1,0:T(8,128)} %get-tuple-element.15.gw_in), custom_call_target="tpu_custom_call" | custom-call | tf_op jit(solution)/shard_map/hand_over/pallas_call | solution.py:529

commit v5 on v4

--- a/solution.py
+++ b/solution.py
@@ -24,8 +24,8 @@
 NT = (((1,), (1,)), ((), ()))
 POS, STATES = 0, 1
 QUERY, STATS, GRAD, PROJ = (2, 3), (4, 5), (6, 7), (8, 9)
-LEFT_X, LEFT_Y, RIGHT_Y, RIGHT_X = (2, 3), (10, 11), (12, 13), (14, 15)
-UNIT, TURNED, OWNERS, WEIGHT = 3, 10, 8, 9
+DIRECT, LEFT, RIGHT = (2, 3), (10, 11), (12, 13)
+UNIT, TURNED, OWNERS, WEIGHT, ACROSS = 3, 10, 8, 9, 11
 STAGES = 16
 HALF = E // 2
 F32, BF16 = jnp.float32, jnp.bfloat16
@@ -35,9 +35,9 @@
     states_ref, w_hbm, bank_hbm, pos_ref,
     loss_ref, top_ref, gs_ref, gw_ref,
     w, bank, posz, posp, stz_out, stz_in, stp_out, slab, turned, turn,
-    zq, zf, unit_s, uz_out, uz_in, qleft, qright, expo, coef, pre, chosen, sp, sz, final, gout, gin,
-    gz_out, gz_in, gs_out, gs_in, gpall, gw_all, gw_in, gw_out, gw_parts, lossbuf,
-    w_sem, bank_sem, cs, cr, zs, zr, ps, pr,
+    zq, zf, unit_s, uz_out, uz_in, qall, expo, coef, pre, chosen, sp, sz, final, gout, gin,
+    gz_out, gz_in, gs_out, gs_in, gpall, gw_all, gw_parts, lossbuf,
+    w_sem, bank_sem, cs, cr, zs, zr, ps, pr, qr,
 ):
     me = lax.axis_index("dev")
     c = lax.rem(me, 2)
@@ -63,29 +63,32 @@
             device_id=(target,), device_id_type=MESH,
         )
 
-    def z_each(body):
-        def step(k, carry):
-            body(lax.rem(z + 4 + (k // 2 + k % 2) * (1 - 2 * (k % 2)), NZ))
-            return carry
-        lax.fori_loop(0, NZ - 1, step, 0)
-
     def away(k):
         return 2 * (1 - k % 2) + (k % 2 + k // 2) % 2
 
-    def p_each(body):
-        def step(k, carry):
-            body(lax.rem(y + away(k // NX), NY) * NX + lax.rem(x + away(k % NX), NX))
-            return carry
-        lax.fori_loop(0, PLANE - 1, step, 0)
+    def each(n, body, short):
+        if short:
+            lax.fori_loop(0, n, lambda k, carry: (body(k), carry)[1], 0)
+        else:
+            for k in range(n):
+                body(k)
+
+    def z_each(body, short=False):
+        each(NZ - 1, lambda k: body(lax.rem(z + 4 + (k // 2 + k % 2) * (1 - 2 * (k % 2)), NZ)), short)
+
+    def p_each(body, short=False):
+        each(PLANE - 1, lambda k: body(
+            lax.rem(y + away(k // NX), NY) * NX + lax.rem(x + away(k % NX), NX)), short)
 
     z_dev = lambda t: dev(y, t, x)
     p_dev = lambda t: dev(t // NX, z, lax.rem(t, NX))
-
-    def z_send(stage, src, dst):
-        z_each(lambda t: copy(src(t), dst(z), zs.at[stage], zr.at[stage], z_dev(t)).start())
-
-    def p_send(stage, src, dst):
-        p_each(lambda t: copy(src(t), dst(p), ps.at[stage], pr.at[stage], p_dev(t)).start())
+    across = lambda t: dev(y, t, x) + 1 - 2 * c
+
+    def z_send(stage, src, dst, short=False):
+        z_each(lambda t: copy(src(t), dst(z), zs.at[stage], zr.at[stage], z_dev(t)).start(), short)
+
+    def p_send(stage, src, dst, short=False):
+        p_each(lambda t: copy(src(t), dst(p), ps.at[stage], pr.at[stage], p_dev(t)).start(), short)
 
     def z_recv(stage, ref, n, base=0):
         part = ref.at[pl.ds(base, (NZ - 1) * n), :]
@@ -119,8 +122,9 @@
         pl.semaphore_signal(barrier, inc=1, device_id=(target,), device_id_type=MESH)
 
     greet(partner)
-    z_each(lambda t: greet(z_dev(t)))
-    p_each(lambda t: greet(p_dev(t)))
+    z_each(lambda t: greet(z_dev(t)), True)
+    z_each(lambda t: greet(across(t)), True)
+    p_each(lambda t: greet(p_dev(t)), True)
     lane = lax.broadcasted_iota(jnp.int32, (8, LANES), 1)
     sub = lax.broadcasted_iota(jnp.int32, (8, LANES), 0)
     own_lane = lax.rem(p, 8) * BLOCK + z
@@ -135,11 +139,11 @@
             at = (yy * NZ + zz) * LANES
             stz_out[pl.ds(zz * 16 + yy, OWN, stride=NY), :] = states_f[:, at:at + LANES]
     stz_in[rows(z, 16), :] = stz_out[rows(z, 16), :]
-    pl.semaphore_wait(barrier, 1 + (NZ - 1) + (PLANE - 1))
+    pl.semaphore_wait(barrier, 1 + 2 * (NZ - 1) + (PLANE - 1))
 
     bank_out = copy(bank_hbm, bank.at[mine, :], cs.at[0], cr.at[0], partner)
-    z_send(POS, lambda t: slots(posz, 8)(z), slots(posz, 8))
-    z_send(STATES, slots(stz_out, 16), slots(stz_in, 16))
+    z_send(POS, lambda t: slots(posz, 8)(z), slots(posz, 8), True)
+    z_send(STATES, slots(stz_out, 16), slots(stz_in, 16), True)
 
     bank_out.start()
     own_bank.start()
@@ -161,14 +165,14 @@
         uz_out[e * 8:e * 8 + OWN, :] = unit[:, e * LANES:(e + 1) * LANES]
         uz_out[e * 8 + OWN:(e + 1) * 8, :] = radius_b
     uz_in[rows(z, 8), :] = uz_out[rows(z, 8), :]
-    z_send(UNIT, slots(uz_out, 8), slots(uz_in, 8))
+    z_send(UNIT, slots(uz_out, 8), slots(uz_in, 8), True)
 
     z_recv(POS, posz, 8)
     tile = jnp.zeros((8, LANES), jnp.int32)
     for s in range(NZ):
         tile = tile + posz[s * 8:(s + 1) * 8, :]
     posp[rows(p, 8), :] = tile
-    p_send(POS, lambda t: slots(posp, 8)(p), slots(posp, 8))
+    p_send(POS, lambda t: slots(posp, 8)(p), slots(posp, 8), True)
     z_recv(STATES, stz_in, 16)
     for yy in range(NY):
         column_slab = [stz_in[pl.ds(r * NY + yy, NZ, stride=16), :] for r in range(OWN)]
@@ -181,35 +185,18 @@
         block = [zf[pl.ds(base + r * SPLIT + e, NZ, stride=step), :] for r in range(PART)]
         return jnp.concatenate(block, axis=0).astype(BF16)
 
-    x_peers = [lax.rem(x + k, NX) for k in (2, 1, 3)]
-    y_peers = [lax.rem(y + k, NY) for k in (2, 1, 3)]
-
-    def p_start(stage, ref, target):
-        copy(ref, ref, ps.at[stage], pr.at[stage], target).start()
+    def q_copy(stage, ref, target, recv_sem):
+        return copy(ref, ref, ps.at[stage], recv_sem, target)
 
     zf[...] = zq[...].astype(F32)
     for s in range(SETS):
-        for e in range(SPLIT // 2):
-            here = slice(e * LANES, (e + 1) * LANES)
-            qleft[s * NY + y, x, :, here] = gathered(s * PART * SPLIT, OWN * SPLIT, e)
-            qright[s * NY + y, x, :, here] = gathered(s * PART * SPLIT, OWN * SPLIT, SPLIT // 2 + e)
-        for i in range(3):
-            p_start(LEFT_X[s], qleft.at[s * NY + y, x], dev(y, z, x_peers[i]))
-            p_start(RIGHT_Y[s], qright.at[s * NY + y, x], dev(y_peers[i], z, x))
-
-    def q_wait(stage, ref):
-        return copy(ref, ref, ps.at[stage], pr.at[stage], partner)
-
-    three_blocks = lambda ref, s: ref.at[s * NY, pl.ds(0, 3)]
-    three_lines = lambda ref, s: ref.at[pl.ds(s * NY, 3)]
-    for s in range(SETS):
-        q_wait(LEFT_X[s], three_blocks(qleft, s)).wait_recv()
-        for i in range(3):
-            p_start(LEFT_Y[s], qleft.at[s * NY + y], dev(y_peers[i], z, x))
-        q_wait(RIGHT_Y[s], three_blocks(qright, s)).wait_recv()
-        for i in range(3):
-            p_start(RIGHT_X[s], qright.at[pl.ds(s * NY, NY), x], dev(y, z, x_peers[i]))
-    p_send(STATES, lambda t: slots(stp_out, 32)(t // NX), slots(slab, 32))
+        for e in range(SPLIT):
+            at = e % (SPLIT // 2) * LANES
+            qall[s * NY + y, x, e // (SPLIT // 2), :, at:at + LANES] = gathered(s * PART * SPLIT, OWN * SPLIT, e)
+        own = qall.at[s * NY + y, x]
+        for k in (2, 1, 3):
+            q_copy(DIRECT[s], own, dev(y, z, lax.rem(x + k, NX)), qr.at[s, k]).start()
+            q_copy(DIRECT[s], own, dev(lax.rem(y + k, NY), z, x), qr.at[s, NX + k]).start()
     own_bank.wait()
     copy(bank.at[other, :], bank.at[other, :], cs.at[0], cr.at[0], partner).wait_recv()
     p_recv(POS, posp, 8)
@@ -227,47 +214,64 @@
     hits_of = lambda s: two_cols(s * 2).astype(jnp.int32)
 
     def pick(s):
-        hit_col = hits_of(s)
+        at = slice(s * SET, (s + 1) * SET)
+        hit_at = hits_of(s) - column
         for j in range(2 * BANK // LANES):
-            coef[:, j * LANES:(j + 1) * LANES] = (column == hit_col - j * LANES).astype(F32).astype(BF16)
+            coef[at, j * LANES:(j + 1) * LANES] = (hit_at == j * LANES).astype(F32).astype(BF16)
         for j in range(E // TILE):
             here = slice(j * TILE, (j + 1) * TILE)
-            chosen[s * SET:(s + 1) * SET, here] = jnp.dot(
-                coef[...], bank[:, here], preferred_element_type=F32).astype(BF16)
+            chosen[at, here] = jnp.dot(coef[at, :], bank[:, here], preferred_element_type=F32).astype(BF16)
 
     pick(0)
+
+    for s in range(SETS):
+        for k in (1, 3, 2):
+            came = qall.at[s * NY + y, lax.rem(x + NX - k, NX)]
+            q_copy(DIRECT[s], came, partner, qr.at[s, k]).wait_recv()
+            for m in (2, 1, 3):
+                q_copy(LEFT[s], came.at[0], dev(lax.rem(y + m, NY), z, x), pr.at[LEFT[s]]).start()
+            came = qall.at[s * NY + lax.rem(y + NY - k, NY), x]
+            q_copy(DIRECT[s], came, partner, qr.at[s, NX + k]).wait_recv()
+            for m in (2, 1, 3):
+                q_copy(RIGHT[s], came.at[1], dev(y, z, lax.rem(x + m, NX)), pr.at[RIGHT[s]]).start()
+
+    p_send(STATES, lambda t: slots(stp_out, 32)(t // NX), slots(slab, 32), True)
     pick(1)
+
+    def q_wait(stage, s):
+        nine = qall.at[pl.ds(s * NY, 3), pl.ds(0, 3), 0]
+        return copy(nine, nine, ps.at[stage], pr.at[stage], partner)
 
     def scores_of(s):
         mine = pl.multiple_of((s * PLANE + p) * 8, 8)
         sp[pl.ds(mine, 8), :] = jnp.zeros((8, LANES), F32)
-        q_wait(LEFT_Y[s], three_lines(qleft, s)).wait_recv()
-        q_wait(RIGHT_X[s], three_lines(qright, s)).wait_recv()
+        q_wait(LEFT[s], s).wait_recv()
+        q_wait(RIGHT[s], s).wait_recv()
         at = slice(s * SET, (s + 1) * SET)
-        left = qleft[s * NY:(s + 1) * NY].reshape(SET, HALF)
-        right = qright[s * NY:(s + 1) * NY].reshape(SET, HALF)
-        hit_col = hits_of(s)
-        groups = [slice(g * LANES, (g + 1) * LANES) for g in range(TILE // LANES)]
-        top, positive = None, jnp.zeros((SET, LANES), F32)
+        left = qall[s * NY:(s + 1) * NY, :, 0].reshape(SET, HALF)
+        right = qall[s * NY:(s + 1) * NY, :, 1].reshape(SET, HALF)
+        hit_at = hits_of(s) - column
+        top = None
         for j in range(tiles):
             here = slice(j * TILE, (j + 1) * TILE)
             scores = 20.0 * (
                 lax.dot_general(left, bank[here, 0:HALF], NT, preferred_element_type=F32)
                 + lax.dot_general(right, bank[here, HALF:E], NT, preferred_element_type=F32)
             )
-            expo[at, here] = scores
-            for g in groups:
-                part = scores[:, g]
+            expo[:, here] = scores
+            for g in range(TILE // LANES):
+                part = scores[:, g * LANES:(g + 1) * LANES]
                 top = part if top is None else jnp.maximum(top, part)
-                positive = positive + jnp.where(column == hit_col - (j * TILE + g.start), part, 0.0)
         top = jnp.max(top, axis=1, keepdims=True)
-        total = jnp.zeros((SET, LANES), F32)
-        for j in range(tiles):
-            here = slice(j * TILE, (j + 1) * TILE)
-            value = jnp.exp(expo[at, here] - top)
-            expo[at, here] = value
-            for g in groups:
-                total = total + value[:, g]
+        total = positive = jnp.zeros((SET, LANES), F32)
+        for j in range(2 * BANK // LANES):
+            here = slice(j * LANES, (j + 1) * LANES)
+            score = expo[:, here]
+            value = jnp.exp(score - top)
+            hit = hit_at == j * LANES
+            total = total + value
+            positive = positive + jnp.where(hit, score, 0.0)
+            coef[at, here] = jnp.where(hit, 0.0, value).astype(BF16)
         total = jnp.sum(total, axis=1, keepdims=True)
         for h in range(2):
             half = slice(h * LANES, (h + 1) * LANES)
@@ -277,6 +281,7 @@
         final[8 + s * 8:16 + s * 8, :] = sp[pl.ds(mine, 8), :]
         at = slots(sp, 8, s * PLANE * 8)
         p_send(STATS[s], lambda t: at(p), at)
+        return jnp.exp(jnp.minimum(jnp.sum(positive, axis=1, keepdims=True) - top, 0.0))
 
     def combine(ref, base, n):
         high = ref[base:base + 8, :]
@@ -313,18 +318,9 @@
 
     def rough_grad(s):
         at = slice(s * SET, (s + 1) * SET)
-        hit_col = hits_of(s)
-        own = jnp.zeros((SET, LANES), F32)
-        for j in range(2 * BANK // LANES):
-            here = slice(j * LANES, (j + 1) * LANES)
-            hit = column == hit_col - j * LANES
-            value = expo[at, here]
-            own = own + jnp.where(hit, value, 0.0)
-            coef[:, here] = jnp.where(hit, 0.0, value).astype(BF16)
         for j in range(E // TILE):
             here = slice(j * TILE, (j + 1) * TILE)
-            pre[at, here] = jnp.dot(coef[...], bank[:, here], preferred_element_type=F32)
-        return jnp.sum(own, axis=1, keepdims=True)
+            pre[at, here] = jnp.dot(coef[at, :], bank[:, here], preferred_element_type=F32)
 
     def grad_of(s, own):
         at = slice(s * SET, (s + 1) * SET)
@@ -337,11 +333,11 @@
         p_send(GRAD[s], slots(gout, BLOCK, s * SET), slots(gin, BLOCK, s * SET))
         gin[rows(p, BLOCK, s * SET), :] = gout[rows(p, BLOCK, s * SET), :]
 
-    scores_of(0)
-    scores_of(1)
-    own_0 = rough_grad(0)
+    own_0 = scores_of(0)
+    own_1 = scores_of(1)
+    rough_grad(0)
     plane_stats(0)
-    own_1 = rough_grad(1)
+    rough_grad(1)
     plane_stats(1)
     lost = all_stats(0)
     grad_of(0, own_0)
@@ -363,7 +359,7 @@
         part = slab[...].astype(F32).reshape(PLANE, 32, LANES)[:, s * BLOCK:(s + 1) * BLOCK, :].reshape(SET, LANES)
         turn[...] = jnp.transpose(part)
         turned[rows(z, 32), s * SET:(s + 1) * SET] = turn[rows(x, 32), :].astype(BF16)
-    z_send(TURNED, lambda t: slots(turned, 32)(z), slots(turned, 32))
+    z_send(TURNED, lambda t: slots(turned, 32)(z), slots(turned, 32), True)
 
     def line_grad(s):
         p_recv(GRAD[s], gin, BLOCK, s * SET)
@@ -372,7 +368,7 @@
             return acc + gin[rows(i, BLOCK, s * SET), :].astype(F32)
 
         acc = lax.fori_loop(0, PLANE, add, jnp.zeros((BLOCK, E), F32))
-        query = jnp.concatenate([qleft[s * NY + y, x], qright[s * NY + y, x]], axis=1).astype(F32)
+        query = jnp.concatenate([qall[s * NY + y, x, 0], qall[s * NY + y, x, 1]], axis=1).astype(F32)
         inner = jnp.sum(query * acc, axis=1, keepdims=True)
         inner = jnp.where(lane == 0, inner[0:NZ, :], jnp.where(lane == 1, inner[NZ:2 * NZ, :], 0.0))
         base = s * NZ * 24
@@ -407,7 +403,7 @@
     z_recv(UNIT, uz_in, 8)
     slice_grad(0)
     slice_grad(1)
-    z_send(OWNERS, slots(gs_out, 8), slots(gs_in, 8))
+    z_send(OWNERS, slots(gs_out, 8), slots(gs_in, 8), True)
     gs_in[rows(z, 8), :] = gs_out[rows(z, 8), :]
 
     z_drain(POS, posz, 8)
@@ -419,10 +415,9 @@
     for s in range(SETS):
         z_drain(STATS[s], sz, 8)
         z_drain(GRAD[s], gz_out, 24)
-        q_wait(LEFT_X[s], three_blocks(qleft, s)).wait_send()
-        q_wait(LEFT_Y[s], three_lines(qleft, s)).wait_send()
-        q_wait(RIGHT_Y[s], three_blocks(qright, s)).wait_send()
-        q_wait(RIGHT_X[s], three_lines(qright, s)).wait_send()
+        q_copy(DIRECT[s], qall.at[pl.ds(s * NY, 2), pl.ds(0, 3)], partner, pr.at[DIRECT[s]]).wait_send()
+        q_wait(LEFT[s], s).wait_send()
+        q_wait(RIGHT[s], s).wait_send()
         p_drain(STATS[s], sp, 8)
         p_drain(GRAD[s], gout, BLOCK)
     bank_out.wait_send()
@@ -434,16 +429,23 @@
     weight = jnp.dot(turned[:, 0:SET], gpall[0:SET, :], preferred_element_type=F32)
     p_recv(PROJ[1], gpall, BLOCK, SET)
     weight = weight + jnp.dot(turned[:, SET:ROWS], gpall[SET:ROWS, :], preferred_element_type=F32)
-    gw_all[...] = weight.reshape(NZ, 32, LANES)
-    core_out = copy(gw_all.at[:, rows(1 - c, 16), :], gw_in, cs.at[2], cr.at[2], partner)
-    core_out.start()
+    gw_all[...] = weight
+    part_of = lambda t, core: gw_all.at[pl.ds(pl.multiple_of(t * 32 + core * 16, 16), 16), :]
+    part_at = gw_parts.at[rows(c * NZ + z, 16), :]
+
+    def cross(t):
+        copy(part_of(t, 1 - c), part_at, zs.at[ACROSS], zr.at[ACROSS], across(t)).start()
+
+    def both(t):
+        copy(part_of(t, c), part_at, zs.at[WEIGHT], zr.at[WEIGHT], z_dev(t)).start()
+        cross(t)
+
+    z_each(both)
+    cross(z)
+    gw_parts[rows(c * NZ + z, 16), :] = gw_all[pl.ds(pl.multiple_of(z * 32 + c * 16, 16), 16), :]
     z_drain(TURNED, turned, 32)
     p_drain(PROJ[0], gpall, BLOCK)
     p_drain(PROJ[1], gpall, BLOCK)
-    core_out.wait()
-    gw_out[...] = (gw_all[:, rows(c, 16), :] + gw_in[...]).reshape(NZ * 16, LANES)
-    z_send(WEIGHT, slots(gw_out, 16), slots(gw_parts, 16))
-    gw_parts[rows(z, 16), :] = gw_out[rows(z, 16), :]
 
     z_recv(OWNERS, gs_in, 8)
     gp = jnp.concatenate([gs_in[e * 8:e * 8 + OWN, :] for e in range(SPLIT)], axis=1).astype(BF16)
@@ -451,10 +453,15 @@
         here = slice(j * TILE, (j + 1) * TILE)
         gs_ref[:, here] = lax.dot_general(gp, w[here, :], NT, preferred_element_type=F32).astype(BF16)
     z_drain(OWNERS, gs_out, 8)
+    eight = gw_parts.at[0:NZ * 16, :]
+    crossed = copy(eight, eight, zs.at[ACROSS], zr.at[ACROSS], partner)
     z_recv(WEIGHT, gw_parts, 16)
+    crossed.wait_recv()
     for e in range(SPLIT):
-        gw_ref[:, e * LANES:(e + 1) * LANES] = gw_parts[e * 16:(e + 1) * 16, :]
-    z_drain(WEIGHT, gw_out, 16)
+        gw_ref[:, e * LANES:(e + 1) * LANES] = (
+            gw_parts[e * 16:(e + 1) * 16, :] + gw_parts[(NZ + e) * 16:(NZ + e + 1) * 16, :])
+    z_drain(WEIGHT, gw_all, 16)
+    crossed.wait_send()
 
 
 def hand_over(loss_in, top_in, gs_in, gw_in, loss_ref, top_ref, gs_ref, gw_ref):
@@ -495,10 +502,9 @@
             vmem((OWN * SPLIT, LANES), F32),
             vmem((NZ * 8, LANES), F32),
             vmem((NZ * 8, LANES), F32),
-            vmem((SETS * NY, NX, BLOCK, HALF), BF16),
-            vmem((SETS * NY, NX, BLOCK, HALF), BF16),
-            vmem((ROWS, 2 * BANK), F32),
-            vmem((SET, 2 * BANK), BF16),
+            vmem((SETS * NY, NX, 2, BLOCK, HALF), BF16),
+            vmem((SET, 2 * BANK), F32),
+            vmem((ROWS, 2 * BANK), BF16),
             vmem((ROWS, E), F32),
             vmem((ROWS, E), BF16),
             vmem((SETS * PLANE * 8, LANES), F32),
@@ -511,15 +517,14 @@
             vmem((NZ * 8, LANES), F32),
             vmem((NZ * 8, LANES), F32),
             vmem((ROWS, LANES), BF16),
-            vmem((NZ, 32, LANES), F32),
-            vmem((NZ, 16, LANES), F32),
-            vmem((NZ * 16, LANES), F32),
-            vmem((NZ * 16, LANES), F32),
+            vmem((NZ * 32, LANES), F32),
+            vmem((2 * NZ * 16, LANES), F32),
             vmem((16, LANES), F32),
             dma((W_PARTS,)), dma,
-            dma((3,)), dma((3,)),
+            dma((2,)), dma((2,)),
             dma((STAGES,)), dma((STAGES,)),
             dma((STAGES,)), dma((STAGES,)),
+            dma((SETS, NX + NY)),
         ],
         compiler_params=pltpu.CompilerParams(
             collective_id=0, has_side_effects=True, vmem_limit_bytes=56 * 2**20

time: 68.3 us -> 67.3 us (0.985)
  Pallas kernels: 67.4 us -> 66.4 us
    pallas_call x1, Pallas kernels: 65.9 us -> 64.9 us  [local(): pl.pallas_call(kernel, out_shape=(jax.ShapeDtypeStruct((8, LANES), F32),)...]
where the time goes in v5:
time: 67.3 us; the launch traced here: 67.1 us
  Pallas kernels  66.4 us (99%)
    pallas_call x1, Pallas kernels, local(): pl.pallas_call(kernel, out_shape=(jax.ShapeDtypeStruct((8, LANES), F32),)...  64.9 us
    pallas_call x1, Pallas kernels, local(): pl.pallas_call(hand_over, out_shape=(jax.ShapeDtypeStruct((1, 1), F32), j...  1.52 us

profile of v5, /device:TPU:1, one launch (start us, length us, event | category | flops | bytes accessed | tf_op | source)
XLA Modules:
  0.0 67.1 jit_solution(11225576056564446660)
XLA Ops:
  0.6 64.9 %info_nce.1 = (f32[8,128]{1,0:T(8,128)}, f32[8,128]{1,0:T(8,128)}, bf16[4,4096]{1,0:T(4,128)(2,1)}, f32[16,1024]{1,0:T(8,128)}) custom-call(bf16[4,4096]{1,0:T(4,128)(2,1)} %states_ref.1, bf16[4096,1024]{1,0:T(8,128)(2,1)} %w_hbm.1, bf16[1024,1024]{1,0:T(8,128)(2,1)} %bank_hbm.1, s32[4]{0:T(128)} %pos_ref.1), custom_call_target="tpu_custom_call" | custom-call | tf_op jit(solution)/shard_map/info_nce/pallas_call | solution.py:479
  65.5 1.5 %hand_over.1 = (f32[1,1]{1,0:T(1,128)}, f32[1,4]{1,0:T(1,128)}, bf16[4,4096]{1,0:T(4,128)(2,1)}, f32[16,1024]{1,0:T(8,128)}) custom-call(f32[8,128]{1,0:T(8,128)} %get-tuple-element.12.loss_in, f32[8,128]{1,0:T(8,128)} %get-tuple-element.13.top_in, bf16[4,4096]{1,0:T(4,128)(2,1)} %get-tuple-element.14.gs_in, f32[16,1024]{1,0:T(8,128)} %get-tuple-element.15.gw_in), custom_call_target="tpu_custom_call" | custom-call | tf_op jit(solution)/shard_map/hand_over/pallas_call | solution.py:534
